TPU v7x, 256 devices: a whole 4x4x8 slice. The times are simulated.
256 devices in a mesh: dp: 4 (over y_lo, core), seq: 8 (over y_hi, x), head: 8 (over z).
Axes of the slice: x: 4, y: 4 (y_hi: 2, y_lo: 2; y = y_hi * 2 + y_lo), z: 8, core: 2. Of those that a mesh axis runs over, the one named last changes fastest.
Arguments:
- queries: bfloat16 [4, 2048, 3072], P('dp', 'seq', 'head'), may hold values from -160 to 160
- key_cache: bfloat16 [4, 2048, 1024], P('dp', 'seq', 'head'), may hold values from -7 to 7
- value_cache: bfloat16 [4, 2048, 1024], P('dp', 'seq', 'head'), may hold values from -6 to 6
- out_grad: bfloat16 [4, 2048, 3072], P('dp', 'seq', 'head'), may hold values from -6 to 6
- doc_ids: int32 [4, 2048], P('dp', 'seq'), may hold values from 0 to 1, never falling along the last dimension, each value on 1 to 2047 neighbouring positions
- layer_input: bfloat16 [4, 2048, 3072], P('dp', ('seq', 'head')), may hold values from -6 to 6
- key_proj: bfloat16 [3072, 1024], P(None, 'head'), may hold values from -0.109375 to 0.109375
- value_proj: bfloat16 [3072, 1024], P(None, 'head'), may hold values from -0.109375 to 0.109375
Outputs:
- query_grad: bfloat16 [4, 2048, 3072], P('dp', 'seq', 'head')
- input_grad: bfloat16 [4, 2048, 3072], P('dp', ('seq', 'head'))
- grad_keyproj: float32 [3072, 1024], P(None, 'head')
- grad_valueproj: float32 [3072, 1024], P(None, 'head')
Inputs may be any that keep to these rules, and one draw needn't show every extreme that they name: `doc_ids`: document numbers never fall along a sequence; a document spans 1 to 2047 positions.
All inputs are finite; a program needn't handle non-finite values.
Results may differ from a plain program's by a relative error of at most 0.02.
Values may be sent and summed in bfloat16 or wider, within the bound.
A program may use at most 64 MiB of HBM per device.

v0:
```python
import jax
import jax.numpy as jnp
from jax import lax
from jax.sharding import PartitionSpec as P

D = 3072
HD = 128
GROUP = 3


NEG_FILL = -1e30


def in_order(tiles, dim):
    shape = list(tiles.shape[1:])
    shape[dim] *= tiles.shape[0]
    return jnp.moveaxis(tiles, 0, dim).reshape(shape)


def sent_to_all(x, axis):
    peers = lax.axis_size(axis)
    return lax.all_to_all(jnp.broadcast_to(x[None], (peers, *x.shape)), axis, 0, 0, tiled=True)


def collect(x, axis, dim):
    return in_order(sent_to_all(x, axis), dim)


def in_blocks(x, dim, peers):
    shape = x.shape
    tiles = x.reshape(*shape[:dim], peers, shape[dim] // peers, *shape[dim + 1 :])
    return jnp.moveaxis(tiles, dim, 0)


def sum_at_owner(x, axis, dim):
    tiles = in_blocks(x, dim, lax.axis_size(axis))
    arrived = lax.all_to_all(tiles, axis, split_axis=0, concat_axis=0, tiled=True)
    return arrived.astype(jnp.float32).sum(axis=0)


def shards(queries, key_cache, value_cache, out_grad, doc_ids, layer_input, key_proj, value_proj):
    rows_query = queries.shape[1]
    col_width = key_cache.shape[2]
    kv_heads = col_width // HD
    cycle_size = lax.axis_size("seq")
    head_count = lax.axis_size("head")
    own_index = lax.axis_index("seq")
    score_scale = HD ** (-0.5)
    query_four = queries[0].reshape(rows_query, kv_heads, GROUP, HD)
    grad_four = out_grad[0].reshape(rows_query, kv_heads, GROUP, HD)
    own_blocks = jnp.stack([key_cache[0], value_cache[0]])
    all_docs = collect(doc_ids, "seq", 1)[0]
    query_doc = doc_ids[0]
    query_pos = own_index * rows_query + lax.iota(jnp.int32, rows_query)
    last_pos = own_index * rows_query + rows_query - 1

    def block_scores(kv_piece, row_start):
        row_total = kv_piece.shape[1]
        key_block = kv_piece[0].reshape(row_total, kv_heads, HD)
        value_block = kv_piece[1].reshape(row_total, kv_heads, HD)
        key_pos = row_start + lax.iota(jnp.int32, row_total)
        key_doc = lax.dynamic_slice_in_dim(all_docs, row_start, row_total)
        allowed = (key_pos[None, :] <= query_pos[:, None]) & (
            key_doc[None, :] == query_doc[:, None]
        )
        scores = (
            jnp.einsum("ihge,jhe->hgij", query_four, key_block, preferred_element_type=jnp.float32)
            * score_scale
        )
        masked = jnp.where(allowed, scores, NEG_FILL)
        weight_grad = jnp.einsum(
            "ihge,jhe->hgij", grad_four, value_block, preferred_element_type=jnp.float32
        )
        return (key_block, allowed, masked, weight_grad)

    def stats_block(state_in, kv_piece, row_start):
        row_top, row_sum, row_acc = state_in
        key_block, allowed, masked, weight_grad = block_scores(kv_piece, row_start)
        new_top = jnp.maximum(row_top, jnp.max(masked, axis=-1))
        weights = jnp.where(allowed, jnp.exp(masked - new_top[..., None]), 0.0)
        decay = jnp.exp(row_top - new_top)
        return (
            new_top,
            row_sum * decay + jnp.sum(weights, axis=-1),
            row_acc * decay + jnp.sum(weights * weight_grad, axis=-1),
        )

    def stats_fold(state_in, kv_piece, row_start):
        row_total = kv_piece.shape[1]
        sub_rows = min(row_total, rows_query)

        def one_part(part_num, state_mid):
            part_start = row_start + part_num * sub_rows
            sub_piece = kv_piece
            return lax.cond(
                part_start <= last_pos,
                lambda: stats_block(state_mid, sub_piece, part_start),
                lambda: state_mid,
            )

        return lax.fori_loop(0, row_total // sub_rows, one_part, state_in)

    stat_shape = (kv_heads, GROUP, rows_query)
    stats_init = (
        jnp.full(stat_shape, NEG_FILL, jnp.float32),
        jnp.zeros(stat_shape, jnp.float32),
        jnp.zeros(stat_shape, jnp.float32),
    )
    all_blocks = collect(own_blocks, "seq", 1)
    row_top, row_sum, row_acc = lax.fori_loop(
        0,
        cycle_size,
        lambda block_num, state_mid: stats_fold(
            state_mid,
            lax.dynamic_slice_in_dim(all_blocks, block_num * rows_query, rows_query, 1),
            block_num * rows_query,
        ),
        stats_init,
    )
    log_total = row_top + jnp.log(row_sum)
    row_delta = row_acc / row_sum

    def grad_block(kv_piece, row_start):
        row_total = kv_piece.shape[1]
        key_block, allowed, masked, weight_grad = block_scores(kv_piece, row_start)
        weights = jnp.where(allowed, jnp.exp(masked - log_total[..., None]), 0.0)
        score_grad = (weights * (weight_grad - row_delta[..., None]) * score_scale).astype(
            jnp.bfloat16
        )
        weights_low = weights.astype(jnp.bfloat16)
        query_add = jnp.einsum(
            "hgij,jhe->ihge", score_grad, key_block, preferred_element_type=jnp.float32
        )
        key_add = jnp.einsum(
            "hgij,ihge->jhe", score_grad, query_four, preferred_element_type=jnp.float32
        )
        value_add = jnp.einsum(
            "hgij,ihge->jhe", weights_low, grad_four, preferred_element_type=jnp.float32
        )
        return (
            query_add,
            jnp.stack(
                [key_add.reshape(row_total, col_width), value_add.reshape(row_total, col_width)]
            ),
        )

    zero_query = jnp.zeros((rows_query, kv_heads, GROUP, HD), jnp.float32)

    def guarded(kv_piece, row_start):
        return lax.cond(
            row_start <= last_pos,
            lambda: grad_block(kv_piece, row_start),
            lambda: (zero_query, jnp.zeros(kv_piece.shape, jnp.float32)),
        )

    def gathered_turn(block_num, state_mid):
        grad_terms, query_sum = state_mid
        row_start = block_num * rows_query
        kv_piece = lax.dynamic_slice_in_dim(all_blocks, row_start, rows_query, 1)
        query_add, kv_add = guarded(kv_piece, row_start)
        return (
            lax.dynamic_update_slice_in_dim(grad_terms, kv_add, row_start, 1),
            query_sum + query_add,
        )

    terms_init = jnp.zeros(all_blocks.shape, jnp.float32)
    grad_terms, query_sum = lax.fori_loop(0, cycle_size, gathered_turn, (terms_init, zero_query))
    kv_grads = sum_at_owner(grad_terms.astype(jnp.bfloat16), "seq", 1)
    query_grad = query_sum.astype(jnp.bfloat16).reshape(1, rows_query, kv_heads * GROUP * HD)
    kv_low = kv_grads.astype(jnp.bfloat16)
    input_rows = rows_query // head_count
    contract_cols = (((1,), (1,)), ((), ()))
    sub_grads = kv_low
    key_term = lax.dot_general(
        sub_grads[0], key_proj, contract_cols, preferred_element_type=jnp.float32
    )
    value_term = lax.dot_general(
        sub_grads[1], value_proj, contract_cols, preferred_element_type=jnp.float32
    )
    input_sum = lax.psum_scatter(
        (key_term + value_term).astype(jnp.bfloat16), "head", scatter_dimension=0, tiled=True
    )
    input_grad = input_sum.reshape(1, input_rows, D)
    contract_rows = (((0,), (0,)), ((), ()))
    input_piece = collect(layer_input[0], "head", 0)
    row_total = input_piece.shape[0]
    sub_grads = kv_low
    key_part = lax.dot_general(
        input_piece, sub_grads[0], contract_rows, preferred_element_type=jnp.float32
    )
    value_part = lax.dot_general(
        input_piece, sub_grads[1], contract_rows, preferred_element_type=jnp.float32
    )
    grad_keyproj, grad_valueproj = (
        lax.psum(key_part.astype(jnp.bfloat16), ("dp", "seq")).astype(jnp.float32),
        lax.psum(value_part.astype(jnp.bfloat16), ("dp", "seq")).astype(jnp.float32),
    )
    return (query_grad, input_grad, grad_keyproj, grad_valueproj)


def solution(mesh):
    return jax.shard_map(
        shards,
        mesh=mesh,
        in_specs=(
            P("dp", "seq", "head"),
            P("dp", "seq", "head"),
            P("dp", "seq", "head"),
            P("dp", "seq", "head"),
            P("dp", "seq"),
            P("dp", ("seq", "head"), None),
            P(None, "head"),
            P(None, "head"),
        ),
        out_specs=(
            P("dp", "seq", "head"),
            P("dp", ("seq", "head"), None),
            P(None, "head"),
            P(None, "head"),
        ),
        check_vma=False,
    )
```

profile of v0, /device:TPU:1, one launch (start us, length us, event | category | flops | bytes accessed | tf_op | source)
XLA Modules:
  0.0 297.8 jit_solution(2051672772160471777)
XLA Ops:
  9.2 23.7 %all_to_all.20 = bf16[8,2,256,128]{3,2,1,0:T(8,128)(2,1)S(1)} all-to-all(bf16[8,2,256,128]{3,2,1,0:T(8,128)(2,1)S(1)} %broadcast_in_dim.75), channel_id=1, replica_groups=mesh['dp'=4,'seq'=8,'head'=8] {'seq'}, dimensions={0} | all-to-all | bytes 2097152 | tf_op jit(solution)/shard_map/all_to_all | solution.py:22
  33.5 3.3 %all-to-all-start.1 = ((s32[8,1,256]{2,1,0:T(1,128)}), s32[8,1,256]{2,1,0:T(1,128)S(1)}, u32[]{:S(2)}, u32[]{:S(2)}) async-start(s32[8,1,256]{2,1,0:T(1,128)} %broadcast_in_dim.77), calls=%async_computation.1 | async-start | bytes 16384 | tf_op jit(solution)/shard_map/all_to_all | solution.py:22
  38.6 4.8 %all-to-all-done.1 = s32[8,1,256]{2,1,0:T(1,128)S(1)} async-done(((s32[8,1,256]{2,1,0:T(1,128)}), s32[8,1,256]{2,1,0:T(1,128)S(1)}, u32[]{:S(2)}, u32[]{:S(2)}) %all-to-all-start.1) | async-done | bytes 8224 | tf_op jit(solution)/shard_map/all_to_all | solution.py:22
  43.3 3.2 %while.49 = (s32[]{:T(128)}, f32[1,3,256]{2,1,0:T(4,128)S(1)}, f32[1,3,256]{2,1,0:T(4,128)S(1)}, f32[1,3,256]{2,1,0:T(4,128)S(1)}, s32[]{:T(128)}, /*index=5*/s3...) while((s32[]{:T(128)}, f32[1,3,256]{2,1,0:T(4,128)S(1)}, ...), condition=%wide.region_6.7_spmd.clone, body=%wide.region_0.6_spmd.clone.sunk | while | flops 102828800 | bytes 3211637 | solution.py:110
  43.4 2.8 conditional.6
  43.6 1.1 fusion.36
  44.8 1.2 fusion.7
  47.6 11.3 %while.50 = (s32[]{:T(128)}, bf16[2,2048,128]{2,1,0:T(8,128)(2,1)}, f32[256,1,3,128]{0,3,2,1:T(8,128)S(1)}, s32[]{:T(128)}, bf16[2,2048,128]{2,1,0:T(8,128)(2,1)...) while((s32[]{:T(128)}, bf16[2,2048,128]{2,1,0:T(8,128)(2,1)}, ...), condition=%wide.region_10.0_spmd.clone, body=%wide.region_7.10_spmd.clone.sunk | while | flops 253886976 | bytes 6900105 | solution.py:167
  47.6 4.2 %conditional.7 = (f32[256,1,3,128]{0,3,2,1:T(8,128)S(1)}, bf16[2,256,128]{2,1,0:T(8,128)(2,1)S(1)}) conditional(s32[]{:T(128)} %convert_element_type.80, () %tuple.114, (bf16[2,2048,128]{2,1,0:T(8,128)(2,1)}, s32[]{:T(128)}, s32[]{:T(128)}, s32[]{:T(128)}, s32[2048]{0:T(1024)S(1)}, /*index=5*/s32[1,256]{1,0:T(1,128)S(1)}, ...), branch_computations={%region_8.8_spmd, %region_9.9_spmd} | conditional | flops 253690368 | bytes 5456462 | solution.py:150
  47.8 1.2 fusion.21
  49.0 1.1 fusion.22
  50.2 1.1 convolution_bitcast_fusion.2
  58.9 1.3 copy.48
  60.2 64.5 %all_to_all.21 = bf16[8,2,256,128]{3,2,1,0:T(8,128)(2,1)} all-to-all(bf16[8,2,256,128]{3,2,1,0:T(8,128)(2,1)S(1)} %copy.48), channel_id=1, replica_groups=mesh['dp'=4,'seq'=8,'head'=8] {'seq'}, dimensions={0} | all-to-all | bytes 2097152 | tf_op jit(solution)/shard_map/all_to_all | solution.py:37
  124.7 1.3 broadcast_in_dim.80
  126.1 8.2 %all-to-all-start.3 = ((bf16[8,32,3072]{2,1,0:T(8,128)(2,1)}), bf16[8,32,3072]{2,1,0:T(8,128)(2,1)S(1)}, u32[]{:S(2)}, u32[]{:S(2)}) async-start(bf16[8,32,3072]{2,1,0:T(8,128)(2,1)} %broadcast_in_dim.80), calls=%async_computation.4 | async-start | bytes 3145728 | tf_op jit(solution)/shard_map/all_to_all | solution.py:22
  134.3 1.4 reduce_sum.34
  135.7 35.8 %all-to-all-done.3 = bf16[8,32,3072]{2,1,0:T(8,128)(2,1)S(1)} async-done(((bf16[8,32,3072]{2,1,0:T(8,128)(2,1)}), bf16[8,32,3072]{2,1,0:T(8,128)(2,1)S(1)}, u32[]{:S(2)}, u32[]{:S(2)}) %all-to-all-start.3) | async-done | bytes 1572896 | tf_op jit(solution)/shard_map/all_to_all | solution.py:22
  171.4 1.3 fusion.33
  172.7 1.3 fusion.34
  175.2 1.7 fusion.32
  177.8 108.5 %all-reduce.3.cloned.1.call-done = (bf16[3072,128]{0,1:T(8,128)(2,1)}, bf16[3072,128]{0,1:T(8,128)(2,1)}) async-done(((bf16[3072,128]{0,1:T(8,128)(2,1)}, bf16[3072,128]{0,1:T(8,128)(2,1)}), (bf16[3072,128]{0,1:T(8,128)(2,1)}, bf16[3072,128]{0,1:T(8,128)(2,1)})) %all-reduce.3.cloned.1.call-update) | async-done | bytes 1572880 | tf_op jit(solution)/shard_map/psum | solution.py:195
  286.3 2.6 copy.50
  289.0 1.4 copy.51
  (109 shorter events, 14.9 us)
Async XLA Ops:
  8.0 166.1 %copy-start = (bf16[3072,128]{1,0:T(8,128)(2,1)S(1)}, bf16[3072,128]{1,0:T(8,128)(2,1)}, u32[]{:S(2)}) copy-start(bf16[3072,128]{1,0:T(8,128)(2,1)} %param.22) | copy-start | bytes 2359300
  9.0 23.9 %copy-start.6 = (s32[1,256]{1,0:T(1,128)S(1)}, s32[1,256]{1,0:T(1,128)}, u32[]{:S(2)}) copy-start(s32[1,256]{1,0:T(1,128)} %param.20) | copy-start | bytes 3076
  9.0 27.9 %copy-start.4 = (bf16[1,256,384]{2,1,0:T(8,128)(2,1)S(1)}, bf16[1,256,384]{2,1,0:T(8,128)(2,1)}, u32[]{:S(2)}) copy-start(bf16[1,256,384]{2,1,0:T(8,128)(2,1)} %param.16) | copy-start | bytes 589828
  9.2 28.0 %copy-start.5 = (bf16[1,256,384]{2,1,0:T(8,128)(2,1)S(1)}, bf16[1,256,384]{2,1,0:T(8,128)(2,1)}, u32[]{:S(2)}) copy-start(bf16[1,256,384]{2,1,0:T(8,128)(2,1)} %param.19) | copy-start | bytes 589828
  33.5 9.8 %all-to-all-start.1 = ((s32[8,1,256]{2,1,0:T(1,128)}), s32[8,1,256]{2,1,0:T(1,128)S(1)}, u32[]{:S(2)}, u32[]{:S(2)}) async-start(s32[8,1,256]{2,1,0:T(1,128)} %broadcast_in_dim.77), calls=%async_computation.1 | async-start | bytes 16384 | tf_op jit(solution)/shard_map/all_to_all | solution.py:22
  60.2 64.5 %copy-start.3 = (bf16[1,32,3072]{2,1,0:T(8,128)(2,1)S(1)}, bf16[1,32,3072]{2,1,0:T(8,128)(2,1)}, u32[]{:S(2)}) copy-start(bf16[1,32,3072]{2,1,0:T(8,128)(2,1)} %param.21) | copy-start | bytes 589828
  126.1 45.4 %all-to-all-start.3 = ((bf16[8,32,3072]{2,1,0:T(8,128)(2,1)}), bf16[8,32,3072]{2,1,0:T(8,128)(2,1)S(1)}, u32[]{:S(2)}, u32[]{:S(2)}) async-start(bf16[8,32,3072]{2,1,0:T(8,128)(2,1)} %broadcast_in_dim.80), calls=%async_computation.4 | async-start | bytes 3145728 | tf_op jit(solution)/shard_map/all_to_all | solution.py:22
  134.2 152.1 %all-reduce.3.cloned.1.call-start = ((), (), s32[]{:S(2)}) async-start(), calls=%async_computation.6 | async-start | bytes 3145728 | tf_op jit(solution)/shard_map/psum | solution.py:195
  174.0 1.1 copy-start.2
  174.0 116.3 %reduce-scatter.2.cloned.1.call-start = ((), (), s32[]{:S(2)}) async-start(), calls=%async_computation.5 | async-start | bytes 1769472 | tf_op jit(solution)/shard_map/reduce_scatter | solution.py:180
  286.3 2.6 copy-start.1
Sparse Core Ops, SparseCore 0:
  174.2 112.1 all-reduce.2
Sparse Core Ops, SparseCore 1:
  177.6 31.8 reduce-scatter.1
where the time goes:
time: 300 us; the launch traced here: 298 us
  waiting for transfers between devices  149 us (50%)
  blocking collectives  88.2 us (29%)
  local copies, waits for them, and re-layouts  17.3 us (6%)
  between operations  15.7 us (5%)
  starting transfers between devices  11.6 us (4%)
  matrix products  11 us (4%)
  other arithmetic  3.81 us (1%)
    psum x1, waiting for transfers between devices, shards(): lax.psum(key_part.astype(jnp.bfloat16), ('dp', 'seq')).astype(jnp.float32)  109 us
    all_to_all x1, blocking collectives, sum_at_owner(): lax.all_to_all(tiles, axis, split_axis=0, concat_axis=0, tiled=True)  64.5 us
    all_to_all x2, waiting for transfers between devices, sent_to_all(): lax.all_to_all(jnp.broadcast_to(x[None], (peers, *x.shape)), axis, 0, 0,...  40.5 us
    all_to_all x1, blocking collectives, sent_to_all(): lax.all_to_all(jnp.broadcast_to(x[None], (peers, *x.shape)), axis, 0, 0,...  23.7 us
    all_to_all x2, starting transfers between devices, sent_to_all(): lax.all_to_all(jnp.broadcast_to(x[None], (peers, *x.shape)), axis, 0, 0,...  11.5 us
  transfers between devices with their start and end apart: 4, of which 3 were waited for; matrix products, arithmetic and copies ran while one was open for 3% of the time, Pallas kernels for 0%

commit v1 on v0

v1 whole, which is shorter than its diff:
```python
import functools
import math

import jax
import jax.numpy as jnp
from jax import lax
from jax.experimental import pallas as pl
from jax.experimental.pallas import tpu as pltpu
from jax.sharding import PartitionSpec as P

D = 3072
HD = 128
GROUP = 3
ROWS = 256
NX = 4
NZ = 8
NEG_FILL = -1e30
SCALE = HD ** (-0.5)
EXP_SCALE = SCALE * math.log2(math.e)
HALF = D // 2
BF = jnp.bfloat16
F32 = jnp.float32
NT = (((1,), (1,)), ((), ()))
NN = (((1,), (0,)), ((), ()))


def dot(a, b, dims):
    return lax.dot_general(a, b, dims, preferred_element_type=F32)


def kernel(
    q_hbm, k_hbm, v_hbm, do_hbm, docs_ref, li_hbm, wk_hbm, wv_hbm,
    qg_hbm, ig_hbm, gp_hbm,
    q_v, do_v, kvbuf, li_buf, li_t, wcat,
    p_buf, dp_buf, m_buf, l_buf, a_buf, f_buf, dq_t,
    gsend, grecv, crecv, xsend, xrecv, acc, kv_low,
    ipart, zs, zr, ig_out,
    csend, ccr, h32, s1, r1, a32, s2, r2, gfull, qg_out,
    loc, kv_ss, kv_rs, li_ss, li_rs, g_ss, g_rs, c_rs, x_sem,
    z_ss, z_rs, core_sem, st1_ss, st1_rs, st2_ss, st2_rs,
    ag1_ss, ag1_rs, ag2_ss, ag2_rs, p_ss, p_rs, out_sem,
):
    dp = lax.axis_index("dp")
    sq = lax.axis_index("seq")
    hd = lax.axis_index("head")
    core = lax.rem(dp, 2)
    y_lo = lax.div(dp, 2)
    y_hi = lax.div(sq, NX)
    x = lax.rem(sq, NX)
    yi = y_hi * 2 + y_lo

    def x_mate(idx):
        return (dp, y_hi * NX + idx, hd)

    def y_mate(idx):
        return (lax.rem(idx, 2) * 2 + core, lax.div(idx, 2) * NX + x, hd)

    other_half = (dp, (1 - y_hi) * NX + x, hd)
    other_core = (y_lo * 2 + 1 - core, sq, hd)
    z_next = (dp, sq, lax.rem(hd + 1, NZ))
    z_prev = (dp, sq, lax.rem(hd + NZ - 1, NZ))

    def remote(src, dst, ssem, rsem, dev):
        return pltpu.make_async_remote_copy(
            src_ref=src, dst_ref=dst, send_sem=ssem, recv_sem=rsem,
            device_id=dev, device_id_type=pl.DeviceIdType.MESH,
        )

    loads = [
        pltpu.make_async_copy(k_hbm, kvbuf.at[sq, pl.ds(0, ROWS), :], loc.at[0]),
        pltpu.make_async_copy(v_hbm, kvbuf.at[sq, pl.ds(ROWS, ROWS), :], loc.at[1]),
        pltpu.make_async_copy(li_hbm, li_buf.at[hd], loc.at[2]),
    ]
    for g in range(GROUP):
        loads.append(pltpu.make_async_copy(q_hbm.at[:, pl.ds(g * HD, HD)], q_v.at[g], loc.at[3 + g]))
        loads.append(pltpu.make_async_copy(do_hbm.at[:, pl.ds(g * HD, HD)], do_v.at[g], loc.at[6 + g]))
    loads.append(pltpu.make_async_copy(wk_hbm, wcat.at[:, pl.ds(0, HD)], loc.at[9]))
    loads.append(pltpu.make_async_copy(wv_hbm, wcat.at[:, pl.ds(HD, HD)], loc.at[10]))
    for c in loads:
        c.start()

    barrier = pltpu.get_barrier_semaphore()
    partners = [x_mate(lax.rem(x + d, NX)) for d in range(1, NX)]
    partners += [y_mate(lax.rem(yi + d, NX)) for d in range(1, NX)]
    partners += [other_core, z_next, z_prev]
    for dev in partners:
        pl.semaphore_signal(barrier, inc=1, device_id=dev, device_id_type=pl.DeviceIdType.MESH)

    doc_row = docs_ref[...].astype(F32)
    upper = lax.broadcasted_iota(jnp.int32, (16, HD), 0) < 8
    doc_tile = jnp.where(
        upper,
        jnp.broadcast_to(doc_row[:, 0:HD], (16, HD)),
        jnp.broadcast_to(doc_row[:, HD:], (16, HD)),
    )
    kvbuf[sq, pl.ds(2 * ROWS, 16), :] = doc_tile.astype(BF)
    m_buf[...] = jnp.full(m_buf.shape, NEG_FILL, F32)
    l_buf[...] = jnp.zeros(l_buf.shape, F32)
    a_buf[...] = jnp.zeros(a_buf.shape, F32)
    dq_t[...] = jnp.zeros(dq_t.shape, F32)
    for c in loads[:3]:
        c.wait()
    pl.semaphore_wait(barrier, len(partners))

    def kv_copy(block, dev, s):
        return remote(kvbuf.at[block], kvbuf.at[block], kv_ss.at[s], kv_rs.at[block], dev)

    @pl.when(y_hi == 0)
    def _():
        kv_copy(sq, other_half, 3).start()

    for d in range(1, NX):
        xt = lax.rem(x + d, NX)

        @pl.when(xt > x)
        def _():
            kv_copy(sq, x_mate(xt), d - 1).start()

    def li_copy(direction, k):
        if direction == 0:
            chunk, dev = lax.rem(hd - k + NZ, NZ), z_next
        else:
            chunk, dev = lax.rem(hd + k, NZ), z_prev
        ref = li_buf.at[chunk]
        if k == 3:
            ref = li_buf.at[chunk, pl.ds(16 * direction, 16), :]
        return remote(ref, ref, li_ss.at[direction, k], li_rs.at[direction, k], dev)

    def li_arrived(direction, k):
        if direction == 0:
            chunk = lax.rem(hd - 1 - k + NZ, NZ)
        else:
            chunk = lax.rem(hd + 1 + k, NZ)
        ref = li_buf.at[chunk]
        if k == 3:
            ref = li_buf.at[chunk, pl.ds(16 * direction, 16), :]
        dev = z_next if direction == 0 else z_prev
        return remote(ref, ref, li_ss.at[direction, k], li_rs.at[direction, k], dev)

    def li_pump(k):
        for direction in range(2):
            li_arrived(direction, k - 1).wait_recv()
        for direction in range(2):
            li_copy(direction, k).start()

    for direction in range(2):
        li_copy(direction, 0).start()

    for c in loads[3:9]:
        c.wait()

    key_iota = lax.broadcasted_iota(jnp.int32, (ROWS, ROWS), 0).astype(F32)

    def score_block(b, diagonal):
        kb = kvbuf[b, pl.ds(0, ROWS), :]
        vb = kvbuf[b, pl.ds(ROWS, ROWS), :]
        docs = kvbuf[b, pl.ds(2 * ROWS, 16), :].astype(F32)
        ones = jnp.sum(jnp.sum(docs, axis=0, keepdims=True), axis=1, keepdims=True) * 0.125
        zeros = ROWS - ones
        low = doc_row * zeros
        high = zeros + doc_row * ones
        if diagonal:
            own = lax.broadcasted_iota(jnp.int32, (1, ROWS), 1).astype(F32)
            high = jnp.minimum(high, own + 1.0)
        allowed = (key_iota >= low) & (key_iota < high)
        for g in range(GROUP):
            s = jnp.where(allowed, dot(kb, q_v[g], NT), NEG_FILL)
            top = jnp.max(s, axis=0, keepdims=True)
            p = jnp.exp2((s - top) * EXP_SCALE)
            wg = dot(vb, do_v[g], NT)
            p_buf[b, g] = p
            dp_buf[b, g] = wg
            m_buf[b, g : g + 1, :] = top
            l_buf[b, g : g + 1, :] = jnp.sum(p, axis=0, keepdims=True)
            a_buf[b, g : g + 1, :] = jnp.sum(p * wg, axis=0, keepdims=True)

    score_block(sq, True)

    @pl.when(y_hi == 1)
    def _():
        kv_copy(x, other_half, 0).wait_recv()
        for d in range(1, NX):
            kv_copy(x, x_mate(lax.rem(x + d, NX)), 3 + d).start()
        score_block(x, False)

    li_pump(1)

    @pl.loop(1, NX)
    def _(d):
        xt = lax.rem(x - d + NX, NX)

        @pl.when(xt < x)
        def _():
            b = y_hi * NX + xt
            kv_copy(b, other_half, 0).wait_recv()
            score_block(b, False)

    li_pump(2)

    @pl.when(y_hi == 1)
    def _():
        @pl.loop(1, NX)
        def _(d):
            b = lax.rem(x - d + NX, NX)
            kv_copy(b, other_half, 0).wait_recv()
            score_block(b, False)

    top = jnp.max(m_buf[...], axis=0)
    factor = jnp.exp2((m_buf[...] - top[None]) * EXP_SCALE)
    total = jnp.sum(factor * l_buf[...], axis=0)
    gathered = jnp.sum(factor * a_buf[...], axis=0)
    safe = jnp.where(total > 0.0, total, 1.0)
    inv = 1.0 / safe
    delta = gathered * inv
    f_buf[...] = factor * inv[None]

    def grad_block(b):
        kbt = kvbuf[b, pl.ds(0, ROWS), :].T
        dk = jnp.zeros((ROWS, HD), F32)
        dv = jnp.zeros((ROWS, HD), F32)
        for g in range(GROUP):
            w = p_buf[b, g] * f_buf[b, g : g + 1, :]
            sg = (w * (dp_buf[b, g] - delta[g : g + 1, :]) * SCALE).astype(BF)
            dv = dv + dot(w.astype(BF), do_v[g], NN)
            dk = dk + dot(sg, q_v[g], NN)
            dq_t[g] += dot(kbt, sg, NN)
        gsend[b, :, 0:HD] = dk.astype(BF)
        gsend[b, :, HD:] = dv.astype(BF)

    def c_copy(d):
        xt = lax.rem(x + d, NX)
        return remote(gsend.at[xt], crecv.at[d - 1], g_ss.at[2 + d], c_rs.at[d - 1], x_mate(xt))

    def g_copy(d):
        xt = lax.rem(x + d, NX)
        return remote(
            gsend.at[y_hi * NX + xt], grecv.at[d - 1], g_ss.at[d - 1], g_rs.at[d - 1], x_mate(xt)
        )

    cross = remote(xsend, xrecv, x_sem.at[0], x_sem.at[1], other_half)

    @pl.when(y_hi == 1)
    def _():
        @pl.loop(1, NX)
        def _(d):
            grad_block(lax.rem(x + d, NX))
            c_copy(d).start()

        grad_block(x)

    @pl.loop(1, NX)
    def _(d):
        xt = lax.rem(x + d, NX)

        @pl.when(xt < x)
        def _():
            grad_block(y_hi * NX + xt)
            g_copy(d).start()

    @pl.when(y_hi == 1)
    def _():
        acc[...] = gsend[x].astype(F32)
        for d in range(1, NX):
            c_copy(d).wait_recv()
            acc[...] += crecv[d - 1].astype(F32)
        xsend[...] = acc[...].astype(BF)
        cross.start()

    grad_block(sq)
    li_pump(3)

    for g in range(GROUP):
        qg_out[:, g * HD : (g + 1) * HD] = dq_t[g].T.astype(BF)
    qg_copy = pltpu.make_async_copy(qg_out, qg_hbm, out_sem.at[0])
    qg_copy.start()

    for direction in range(2):
        li_arrived(direction, 3).wait_recv()

    for n in range(D // 512):
        cols = li_buf[:, :, n * 512 : (n + 1) * 512].reshape(ROWS, 512)
        li_t[n * 512 : (n + 1) * 512, :] = cols.T

    for c in loads[9:]:
        c.wait()

    acc[...] = gsend[sq].astype(F32)

    for d in range(1, NX):
        @pl.when(lax.rem(x - d + NX, NX) > x)
        def _():
            g_copy(d).wait_recv()
            acc[...] += grecv[d - 1].astype(F32)

    @pl.when(y_hi == 0)
    def _():
        cross.wait_recv()
        acc[...] += xrecv[...].astype(F32)

    kv_low[...] = acc[...].astype(BF)

    for n in range(D // 512):
        part = dot(kv_low[...], wcat[n * 512 : (n + 1) * 512, :], NT)
        ipart[:, :, n * 512 : (n + 1) * 512] = part.reshape(NZ, 32, 512)

    def z_copy(direction, k, half):
        return remote(
            zs.at[direction, k, half], zr.at[direction, k, half],
            z_ss.at[direction, k, half], z_rs.at[direction, k, half],
            z_next if direction == 0 else z_prev,
        )

    def z_send(direction, k, half, add):
        t = lax.rem(hd + 4 - k, NZ) if direction == 0 else lax.rem(hd + 4 + k, NZ)
        term = ipart[t, :, half * HALF : (half + 1) * HALF]
        if add:
            z_copy(direction, k - 1, half).wait_recv()
            term = term + zr[direction, k - 1, half].astype(F32)
        zs[direction, k, half] = term.astype(BF)
        z_copy(direction, k, half).start()

    z_send(0, 0, 0, False)
    z_send(1, 0, 1, False)
    z_send(0, 1, 1, False)
    z_send(1, 1, 0, False)

    low = kv_low[...]
    for n in range(3):
        rows = pl.ds(pl.multiple_of((1 - core) * HALF + n * 512, 512), 512)
        csend[n * 512 : (n + 1) * 512, :] = dot(li_t[rows, :], low, NN).astype(BF)
    core_copy = remote(csend, ccr, core_sem.at[0], core_sem.at[1], other_core)
    core_copy.start()
    for n in range(3):
        rows = pl.ds(pl.multiple_of(core * HALF + n * 512, 512), 512)
        h32[n * 512 : (n + 1) * 512, :] = dot(li_t[rows, :], low, NN)

    z_send(0, 1, 0, True)
    z_send(1, 1, 1, True)

    core_copy.wait_recv()
    for n in range(8):
        rows = pl.ds(n * 192, 192)
        total_n = h32[rows, :] + ccr[rows, :].astype(F32)
        h32[rows, :] = total_n
        s1[n // 4, n % 4] = total_n.astype(BF)

    def mate(stage, part, d):
        if (stage + part) % 2 == 0:
            return x_mate(lax.rem(x + d, NX))
        return y_mate(lax.rem(yi + d, NX))

    own1 = (x, yi)
    own2 = (yi, x)

    def st1_copy(part, d):
        to = lax.rem(own1[part] + d, NX)
        return remote(
            s1.at[part, to], r1.at[part, d - 1], st1_ss.at[part, d - 1], st1_rs.at[part, d - 1],
            mate(0, part, d),
        )

    def st2_copy(part, d):
        to = lax.rem(own2[part] + d, NX)
        return remote(
            s2.at[part, to], r2.at[part, d - 1], st2_ss.at[part, d - 1], st2_rs.at[part, d - 1],
            mate(1, part, d),
        )

    for d in (2, 1, 3):
        for part in range(2):
            st1_copy(part, d).start()

    for half in (1, 0):
        z_send(0, 2, half, True)
        z_send(1, 2, 1 - half, True)

    for part in range(2):
        base = pl.multiple_of(part * 768 + own1[part] * 192, 192)
        term = h32[pl.ds(base, 192), :]
        for d in range(1, NX):
            st1_copy(part, d).wait_recv()
            term = term + r1[part, d - 1].astype(F32)
        term = term.reshape(NX, 48, 2 * HD)
        a32[part] = term
        s2[part] = term.astype(BF)
        for d in (2, 1, 3):
            st2_copy(part, d).start()

    for half in (1, 0):
        z_send(0, 3, half, True)
        z_send(1, 3, 1 - half, True)

    def full(c, part, i, j):
        return gfull.at[c, part, i, j]

    def ag1_copy(part, d):
        ref = full(core, part, own1[part], own2[part])
        return remote(ref, ref, ag1_ss.at[part, d - 1], ag1_rs.at[part, d - 1], mate(1, part, d))

    def ag1_arrived(part, d):
        ref = full(core, part, own1[part], lax.rem(own2[part] - d + NX, NX))
        return remote(ref, ref, ag1_ss.at[part, d - 1], ag1_rs.at[part, d - 1], mate(1, part, d))

    def ag2_copy(part, d):
        ref = gfull.at[core, part, own1[part]]
        return remote(ref, ref, ag2_ss.at[part, d - 1], ag2_rs.at[part, d - 1], mate(0, part, d))

    def ag2_arrived(part, d):
        ref = gfull.at[core, part, lax.rem(own1[part] - d + NX, NX)]
        return remote(ref, ref, ag2_ss.at[part, d - 1], ag2_rs.at[part, d - 1], mate(0, part, d))

    def pair_copy(part, d):
        ref = gfull.at[core, part, lax.rem(own1[part] - d + NX, NX)]
        return remote(ref, ref, p_ss.at[part, d], p_rs.at[part, d], other_core)

    def pair_arrived(part, d):
        ref = gfull.at[1 - core, part, lax.rem(own1[part] - d + NX, NX)]
        return remote(ref, ref, p_ss.at[part, d], p_rs.at[part, d], other_core)

    for part in range(2):
        term = a32[part, own2[part]]
        for d in range(1, NX):
            st2_copy(part, d).wait_recv()
            term = term + r2[part, d - 1].astype(F32)
        gfull[core, part, own1[part], own2[part]] = term.astype(BF)
        for d in (2, 1, 3):
            ag1_copy(part, d).start()

    for part in range(2):
        for d in range(1, NX):
            ag1_arrived(part, d).wait_recv()
        for d in (2, 1, 3):
            ag2_copy(part, d).start()
        pair_copy(part, 0).start()

    for part in range(2):
        for d in (1, 3, 2):
            ag2_arrived(part, d).wait_recv()
            pair_copy(part, d).start()

    for half in range(2):
        term = ipart[hd, :, half * HALF : (half + 1) * HALF]
        for direction in range(2):
            z_copy(direction, 3, half).wait_recv()
            term = term + zr[direction, 3, half].astype(F32)
        ig_out[:, half * HALF : (half + 1) * HALF] = term.astype(BF)
    ig_copy = pltpu.make_async_copy(ig_out, ig_hbm, out_sem.at[1])
    ig_copy.start()

    for part in range(2):
        for d in range(NX):
            pair_arrived(part, d).wait_recv()
    gp_copy = pltpu.make_async_copy(gfull, gp_hbm, out_sem.at[2])
    gp_copy.start()

    @pl.when(y_hi == 0)
    def _():
        kv_copy(sq, other_half, 3).wait_send()

    for d in range(1, NX):
        xt = lax.rem(x + d, NX)

        @pl.when(xt > x)
        def _():
            kv_copy(sq, x_mate(xt), d - 1).wait_send()

        @pl.when(xt < x)
        def _():
            g_copy(d).wait_send()

    @pl.when(y_hi == 1)
    def _():
        for d in range(1, NX):
            kv_copy(x, x_mate(lax.rem(x + d, NX)), 3 + d).wait_send()
            c_copy(d).wait_send()
        cross.wait_send()

    for direction in range(2):
        for k in range(4):
            li_copy(direction, k).wait_send()
            for half in range(2):
                if k > 0 or half == direction:
                    z_copy(direction, k, half).wait_send()
    core_copy.wait_send()
    for part in range(2):
        for d in range(1, NX):
            st1_copy(part, d).wait_send()
            st2_copy(part, d).wait_send()
            ag1_copy(part, d).wait_send()
            ag2_copy(part, d).wait_send()
        for d in range(NX):
            pair_copy(part, d).wait_send()
    qg_copy.wait()
    ig_copy.wait()
    gp_copy.wait()


def shards(queries, key_cache, value_cache, out_grad, doc_ids, layer_input, key_proj, value_proj):
    hbm = pl.BlockSpec(memory_space=pl.ANY)
    vmem = pl.BlockSpec(memory_space=pltpu.VMEM)
    dma = pltpu.SemaphoreType.DMA
    scratch = [
        pltpu.VMEM((GROUP, ROWS, HD), BF),
        pltpu.VMEM((GROUP, ROWS, HD), BF),
        pltpu.VMEM((8, 2 * ROWS + 16, HD), BF),
        pltpu.VMEM((NZ, 32, D), BF),
        pltpu.VMEM((D, ROWS), BF),
        pltpu.VMEM((D, 2 * HD), BF),
        pltpu.VMEM((8, GROUP, ROWS, ROWS), F32),
        pltpu.VMEM((8, GROUP, ROWS, ROWS), F32),
        pltpu.VMEM((8, 8, ROWS), F32),
        pltpu.VMEM((8, 8, ROWS), F32),
        pltpu.VMEM((8, 8, ROWS), F32),
        pltpu.VMEM((8, 8, ROWS), F32),
        pltpu.VMEM((GROUP, HD, ROWS), F32),
        pltpu.VMEM((8, ROWS, 2 * HD), BF),
        pltpu.VMEM((3, ROWS, 2 * HD), BF),
        pltpu.VMEM((3, ROWS, 2 * HD), BF),
        pltpu.VMEM((ROWS, 2 * HD), BF),
        pltpu.VMEM((ROWS, 2 * HD), BF),
        pltpu.VMEM((ROWS, 2 * HD), F32),
        pltpu.VMEM((ROWS, 2 * HD), BF),
        pltpu.VMEM((NZ, 32, D), F32),
        pltpu.VMEM((2, 4, 2, 32, HALF), BF),
        pltpu.VMEM((2, 4, 2, 32, HALF), BF),
        pltpu.VMEM((32, D), BF),
        pltpu.VMEM((HALF, 2 * HD), BF),
        pltpu.VMEM((HALF, 2 * HD), BF),
        pltpu.VMEM((HALF, 2 * HD), F32),
        pltpu.VMEM((2, NX, 192, 2 * HD), BF),
        pltpu.VMEM((2, 3, 192, 2 * HD), BF),
        pltpu.VMEM((2, NX, 48, 2 * HD), F32),
        pltpu.VMEM((2, NX, 48, 2 * HD), BF),
        pltpu.VMEM((2, 3, 48, 2 * HD), BF),
        pltpu.VMEM((2, 2, NX, NX, 48, 2 * HD), BF),
        pltpu.VMEM((ROWS, GROUP * HD), BF),
        dma((11,)),
        dma((7,)),
        dma((8,)),
        dma((2, 4)),
        dma((2, 4)),
        dma((6,)),
        dma((3,)),
        dma((3,)),
        dma((2,)),
        dma((2, 4, 2)),
        dma((2, 4, 2)),
        dma((2,)),
        dma((2, 3)),
        dma((2, 3)),
        dma((2, 3)),
        dma((2, 3)),
        dma((2, 3)),
        dma((2, 3)),
        dma((2, 3)),
        dma((2, 3)),
        dma((2, 4)),
        dma((2, 4)),
        dma((3,)),
    ]
    qg, ig, gp = pl.pallas_call(
        kernel,
        out_shape=(
            jax.ShapeDtypeStruct((ROWS, GROUP * HD), BF),
            jax.ShapeDtypeStruct((32, D), BF),
            jax.ShapeDtypeStruct((2, 2, NX, NX, 48, 2 * HD), BF),
        ),
        in_specs=[hbm, hbm, hbm, hbm, vmem, hbm, hbm, hbm],
        out_specs=(hbm, hbm, hbm),
        scratch_shapes=scratch,
        compiler_params=pltpu.CompilerParams(
            collective_id=0, has_side_effects=True, vmem_limit_bytes=56 * 1024 * 1024
        ),
        cost_estimate=pl.CostEstimate(
            flops=3 * 10**9, bytes_accessed=8 * 10**6, transcendentals=2 * 10**6
        ),
    )(
        queries[0], key_cache[0], value_cache[0], out_grad[0], doc_ids, layer_input[0],
        key_proj, value_proj,
    )
    grads = gp.reshape(D, 2 * HD)
    return (
        qg[None],
        ig[None],
        grads[:, :HD].astype(F32),
        grads[:, HD:].astype(F32),
    )


def solution(mesh):
    return jax.shard_map(
        shards,
        mesh=mesh,
        in_specs=(
            P("dp", "seq", "head"),
            P("dp", "seq", "head"),
            P("dp", "seq", "head"),
            P("dp", "seq", "head"),
            P("dp", "seq"),
            P("dp", ("seq", "head"), None),
            P(None, "head"),
            P(None, "head"),
        ),
        out_specs=(
            P("dp", "seq", "head"),
            P("dp", ("seq", "head"), None),
            P(None, "head"),
            P(None, "head"),
        ),
        check_vma=False,
    )
```

time: 300 us -> 75 us (0.25)
  waiting for transfers between devices: 149 us -> 0 us
  blocking collectives: 88.2 us -> 0 us
  Pallas kernels: 0 us -> 69.6 us
  local copies, waits for them, and re-layouts: 17.3 us -> 1.36 us
  between operations: 15.7 us -> 0.66 us
  starting transfers between devices: 11.6 us -> 0 us
  matrix products: 11 us -> 0 us
    psum x1 -> x0, waiting for transfers between devices: 109 us -> none  [shards(): lax.psum(key_part.astype(jnp.bfloat16), ('dp', 'seq')).astype(jnp.float32)]
    all_to_all x2 -> x0, blocking collectives: 88.2 us -> none  [the longest x1 64.5 us: sum_at_owner(): lax.all_to_all(tiles, axis, split_axis=0, concat_axis=0, tiled=True)]
    pallas_call x0 -> x1, Pallas kernels: none -> 69.6 us  [shards(): pl.pallas_call(kernel, out_shape=(jax.ShapeDtypeStruct((ROWS, GROUP * HD)...]
    all_to_all x2 -> x0, waiting for transfers between devices: 40.5 us -> none  [sent_to_all(): lax.all_to_all(jnp.broadcast_to(x[None], (peers, *x.shape)), axis, 0, 0,...]
    all_to_all x2 -> x0, starting transfers between devices: 11.5 us -> none  [sent_to_all(): lax.all_to_all(jnp.broadcast_to(x[None], (peers, *x.shape)), axis, 0, 0,...]
    dot_general x11 -> x0, matrix products: 11 us -> none  [the longest x2 2.33 us: block_scores(): jnp.einsum('ihge,jhe->hgij', query_four, key_block, preferred_element_typ...]
    dynamic_update_slice x8 -> x0, local copies, waits for them, and re-layouts: 5.37 us -> none  [gathered_turn(): lax.dynamic_update_slice_in_dim(grad_terms, kv_add, row_start, 1)]
    unnamed x21 -> x6, local copies, waits for them, and re-layouts: 6 us -> 1.36 us
  transfers between devices with their start and end apart: 4 -> 0, of which waited for: 3 -> 0; matrix products, arithmetic and copies ran while one was open for 3% -> 0% of each run, Pallas kernels for 0% -> 0%
where the time goes in v1:
time: 75 us; the launch traced here: 74.9 us
  Pallas kernels  69.6 us (93%)
  other arithmetic  3.28 us (4%)
  local copies, waits for them, and re-layouts  1.36 us (2%)
    pallas_call x1, Pallas kernels, shards(): pl.pallas_call(kernel, out_shape=(jax.ShapeDtypeStruct((ROWS, GROUP * HD)...  69.6 us
    convert_element_type x1, other arithmetic, shards(): grads[:, HD:].astype(F32)  3.28 us

profile of v1, /device:TPU:1, one launch (start us, length us, event | category | flops | bytes accessed | tf_op | source)
XLA Modules:
  0.0 74.9 jit_solution(3740487410975883993)
XLA Ops:
  0.6 69.6 %shard_map.111 = (bf16[256,384]{1,0:T(8,128)(2,1)}, bf16[32,3072]{1,0:T(8,128)(2,1)}, bf16[2,2,4,4,48,256]{5,4,3,2,1,0:T(8,128)(2,1)}) custom-call(bf16[256,384]{1,0:T(8,128)(2,1)} %bitcast.11, bf16[256,128]{1,0:T(8,128)(2,1)} %bitcast.14, bf16[256,128]{1,0:T(8,128)(2,1)} %bitcast.15, bf16[256,384]{1,0:T(8,128)(2,1)} %bitcast.12, s32[1,256]{1,0:T(1,128)} %docs_ref.1, ...), custom_call_target="tpu_custom_call" | custom-call | flops 3000000000 | bytes 8000000 | tf_op jit(solution)/shard_map/pallas_call | solution.py:561
  70.2 0.0 copy-start.1
  70.2 0.0 copy-start
  70.2 3.3 %slice_convert_fusion = (f32[3072,128]{1,0:T(8,128)}, f32[3072,128]{1,0:T(8,128)}) fusion(bf16[3072,256]{1,0:T(8,128)(2,1)} %bitcast.8), kind=kLoop, calls=%fused_computation | loop fusion | flops 786432 | bytes 4718592 | tf_op jit(solution)/shard_map/convert_element_type | solution.py:586
  73.5 0.0 copy-done.1
  73.5 0.7 copy.14
  74.2 0.0 copy-done
  74.2 0.7 copy.15
Async XLA Ops:
  70.2 3.3 %copy-start.1 = (bf16[256,384]{1,0:T(8,128)(2,1)S(1)}, bf16[256,384]{1,0:T(8,128)(2,1)}, u32[]{:S(2)}) copy-start(bf16[256,384]{1,0:T(8,128)(2,1)} %get-tuple-element.7) | copy-start | bytes 589828
  70.2 4.0 %copy-start = (bf16[32,3072]{1,0:T(8,128)(2,1)S(1)}, bf16[32,3072]{1,0:T(8,128)(2,1)}, u32[]{:S(2)}) copy-start(bf16[32,3072]{1,0:T(8,128)(2,1)} %get-tuple-element.8) | copy-start | bytes 589828

commit v2 on v1

v2 whole, which is shorter than its diff:
```python
import functools
import math

import jax
import jax.numpy as jnp
from jax import lax
from jax.experimental import pallas as pl
from jax.experimental.pallas import tpu as pltpu
from jax.sharding import PartitionSpec as P

D = 3072
HD = 128
GROUP = 3
ROWS = 256
NX = 4
NZ = 8
NEG_FILL = -1e30
SCALE = HD ** (-0.5)
EXP_SCALE = SCALE * math.log2(math.e)
HALF = D // 2
NS = 8
PARTS = 4
PART = HALF // PARTS
SUB = PART // NX
PIECES = 4
BF = jnp.bfloat16
F32 = jnp.float32
NT = (((1,), (1,)), ((), ()))
NN = (((1,), (0,)), ((), ()))


def dot(a, b, dims):
    return lax.dot_general(a, b, dims, preferred_element_type=F32)


def kernel(
    q_hbm, k_hbm, v_hbm, do_hbm, docs_hbm, li_hbm, wk_hbm, wv_hbm,
    qg_hbm, ig_hbm, gp_hbm,
    q_v, do_v, docs_ref, kvbuf, li_buf, li_t, wcat,
    p_buf, dp_buf, m_buf, l_buf, a_buf, f_buf, dq_t,
    gsend, grecv, acc, kv_low,
    ipart, zs, zr, ig_out,
    csend, ccr, h32, s1, r1, r2, gfull, qg_out,
    loc, kv_ss, kv_rs, li_ss, li_rs, g_ss, g_rs,
    z_ss, z_rs, core_ss, core_rs, st1_ss, st1_rs, st2_ss, st2_rs,
    ag_ss, ag_rs, p_ss, p_rs, out_sem,
):
    dp = lax.axis_index("dp")
    sq = lax.axis_index("seq")
    hd = lax.axis_index("head")
    core = lax.rem(dp, 2)
    y_lo = lax.div(dp, 2)
    y_hi = lax.div(sq, NX)
    x = lax.rem(sq, NX)
    yi = y_hi * 2 + y_lo

    def seq_mate(idx):
        return (dp, idx, hd)

    def x_mate(idx):
        return (dp, y_hi * NX + idx, hd)

    def y_mate(idx):
        return (lax.rem(idx, 2) * 2 + core, lax.div(idx, 2) * NX + x, hd)

    other_core = (y_lo * 2 + 1 - core, sq, hd)

    def z_mate(d):
        return (dp, sq, lax.rem(hd + d + NZ, NZ))

    def remote(src, dst, ssem, rsem, dev):
        return pltpu.make_async_remote_copy(
            src_ref=src, dst_ref=dst, send_sem=ssem, recv_sem=rsem,
            device_id=dev, device_id_type=pl.DeviceIdType.MESH,
        )

    barrier = pltpu.get_barrier_semaphore()
    partners = [seq_mate(lax.rem(sq + d, NS)) for d in range(1, NS)]
    partners += [y_mate(lax.rem(yi + d, NX)) for d in (1, 3)]
    partners += [other_core, z_mate(1), z_mate(-1), z_mate(2), z_mate(-2)]
    for dev in partners:
        pl.semaphore_signal(barrier, inc=1, device_id=dev, device_id_type=pl.DeviceIdType.MESH)

    loads = [
        pltpu.make_async_copy(docs_hbm, docs_ref, loc.at[0]),
        pltpu.make_async_copy(k_hbm, kvbuf.at[sq, pl.ds(0, ROWS), :], loc.at[1]),
        pltpu.make_async_copy(v_hbm, kvbuf.at[sq, pl.ds(ROWS, ROWS), :], loc.at[2]),
        pltpu.make_async_copy(li_hbm, li_buf.at[hd], loc.at[3]),
    ]
    for g in range(GROUP):
        loads.append(pltpu.make_async_copy(q_hbm.at[:, pl.ds(g * HD, HD)], q_v.at[g], loc.at[4 + g]))
        loads.append(pltpu.make_async_copy(do_hbm.at[:, pl.ds(g * HD, HD)], do_v.at[g], loc.at[7 + g]))
    loads.append(pltpu.make_async_copy(wk_hbm, wcat.at[:, pl.ds(0, HD)], loc.at[10]))
    loads.append(pltpu.make_async_copy(wv_hbm, wcat.at[:, pl.ds(HD, HD)], loc.at[11]))
    for c in loads:
        c.start()

    m_buf[...] = jnp.full(m_buf.shape, NEG_FILL, F32)
    l_buf[...] = jnp.zeros(l_buf.shape, F32)
    a_buf[...] = jnp.zeros(a_buf.shape, F32)
    dq_t[...] = jnp.zeros(dq_t.shape, F32)

    loads[0].wait()
    doc_row = docs_ref[...].astype(F32)
    upper = lax.broadcasted_iota(jnp.int32, (16, HD), 0) < 8
    doc_tile = jnp.where(
        upper,
        jnp.broadcast_to(doc_row[:, 0:HD], (16, HD)),
        jnp.broadcast_to(doc_row[:, HD:], (16, HD)),
    )
    kvbuf[sq, pl.ds(2 * ROWS, 16), :] = doc_tile.astype(BF)
    for c in loads[1:4]:
        c.wait()
    pl.semaphore_wait(barrier, len(partners))

    def kv_copy(block, dev, s):
        return remote(kvbuf.at[block], kvbuf.at[block], kv_ss.at[s], kv_rs.at[block], dev)

    def kv_arrived(block):
        return kv_copy(block, seq_mate(lax.rem(sq + 1, NS)), 0)

    for d in range(NS - 1, 0, -1):

        @pl.when(sq + d < NS)
        def _():
            kv_copy(sq, seq_mate(sq + d), d - 1).start()

    li_moves = ((1, 0, (0, 32)), (2, 0, (0, 16)), (1, 1, (16, 16)), (2, 1, (0, 16)), (1, 2, (16, 16)), None)

    def li_copy(direction, n, arrived=False):
        hops, away, (row, size) = li_moves[n] or (2, 2, (16 * direction, 16))
        sign = 1 - 2 * direction
        away = away + hops if arrived else away
        ref = li_buf.at[lax.rem(hd - sign * away + NZ, NZ), pl.ds(row, size), :]
        return remote(ref, ref, li_ss.at[direction, n], li_rs.at[direction, n], z_mate(sign * hops))

    def li_start(*moves):
        for n in moves:
            for direction in range(2):
                li_copy(direction, n).start()

    def li_wait(*moves):
        for n in moves:
            for direction in range(2):
                li_copy(direction, n, True).wait_recv()

    li_start(0, 1)

    for c in loads[4:10]:
        c.wait()

    key_iota = lax.broadcasted_iota(jnp.int32, (ROWS, ROWS), 0).astype(F32)

    def score_block(b, diagonal):
        kb = kvbuf[b, pl.ds(0, ROWS), :]
        vb = kvbuf[b, pl.ds(ROWS, ROWS), :]
        docs = kvbuf[b, pl.ds(2 * ROWS, 16), :].astype(F32)
        ones = jnp.sum(jnp.sum(docs, axis=0, keepdims=True), axis=1, keepdims=True) * 0.125
        zeros = ROWS - ones
        low = doc_row * zeros
        high = zeros + doc_row * ones
        if diagonal:
            own = lax.broadcasted_iota(jnp.int32, (1, ROWS), 1).astype(F32)
            high = jnp.minimum(high, own + 1.0)
        allowed = (key_iota >= low) & (key_iota < high)
        for g in range(GROUP):
            s = jnp.where(allowed, dot(kb, q_v[g], NT), NEG_FILL)
            top = jnp.max(s, axis=0, keepdims=True)
            p = jnp.exp2((s - top) * EXP_SCALE)
            wg = dot(vb, do_v[g], NT)
            p_buf[b, g] = p
            dp_buf[b, g] = wg
            m_buf[b, g : g + 1, :] = top
            l_buf[b, g : g + 1, :] = jnp.sum(p, axis=0, keepdims=True)
            a_buf[b, g : g + 1, :] = jnp.sum(p * wg, axis=0, keepdims=True)

    score_block(sq, True)

    @pl.loop(1, NX)
    def _(d):
        @pl.when(d <= x)
        def _():
            kv_arrived(sq - d).wait_recv()
            score_block(sq - d, False)

    li_wait(0)
    li_start(2, 3)

    @pl.when(y_hi == 1)
    def _():
        @pl.loop(0, NX)
        def _(d):
            kv_arrived(NX - 1 - d).wait_recv()
            score_block(NX - 1 - d, False)

    top = jnp.max(m_buf[...], axis=0)
    factor = jnp.exp2((m_buf[...] - top[None]) * EXP_SCALE)
    total = jnp.sum(factor * l_buf[...], axis=0)
    gathered = jnp.sum(factor * a_buf[...], axis=0)
    safe = jnp.where(total > 0.0, total, 1.0)
    inv = 1.0 / safe
    delta = gathered * inv
    f_buf[...] = factor * inv[None]

    def grad_block(b):
        kbt = kvbuf[b, pl.ds(0, ROWS), :].T
        dk = jnp.zeros((ROWS, HD), F32)
        dv = jnp.zeros((ROWS, HD), F32)
        for g in range(GROUP):
            w = p_buf[b, g] * f_buf[b, g : g + 1, :]
            sg = (w * (dp_buf[b, g] - delta[g : g + 1, :]) * SCALE).astype(BF)
            dv = dv + dot(w.astype(BF), do_v[g], NN)
            dk = dk + dot(sg, q_v[g], NN)
            dq_t[g] += dot(kbt, sg, NN)
        gsend[b, :, 0:HD] = dk.astype(BF)
        gsend[b, :, HD:] = dv.astype(BF)

    def g_copy(d):
        return remote(
            gsend.at[sq - d], grecv.at[d - 1], g_ss.at[d - 1], g_rs.at[d - 1], seq_mate(sq - d)
        )

    def g_arrived(d):
        return remote(
            gsend.at[sq], grecv.at[d - 1], g_ss.at[d - 1], g_rs.at[d - 1], seq_mate(sq + d)
        )

    @pl.loop(0, NS - 1)
    def _(b):
        @pl.when(b < sq)
        def _():
            grad_block(b)
            g_copy(sq - b).start()

    li_wait(1, 2)
    li_start(4, 5)

    grad_block(sq)

    for g in range(GROUP):
        qg_out[:, g * HD : (g + 1) * HD] = dq_t[g].T.astype(BF)
    qg_copy = pltpu.make_async_copy(qg_out, qg_hbm, out_sem.at[0])
    qg_copy.start()

    for c in loads[10:]:
        c.wait()

    acc[...] = gsend[sq].astype(F32)

    @pl.loop(1, NS)
    def _(d):
        @pl.when(sq + d < NS)
        def _():
            g_arrived(d).wait_recv()
            acc[...] += grecv[d - 1].astype(F32)

    kv_low[...] = acc[...].astype(BF)

    li_wait(3, 4, 5)
    for n in range(D // 512):
        cols = li_buf[:, :, n * 512 : (n + 1) * 512].reshape(ROWS, 512)
        li_t[n * 512 : (n + 1) * 512, :] = cols.T

    def core_copy(p):
        return remote(csend.at[p], ccr.at[p], core_ss.at[p], core_rs.at[p], other_core)

    def proj_part(which, p):
        rows = pl.ds(pl.multiple_of(which * HALF + p * PART, PART), PART)
        return dot(li_t[rows, :], kv_low[...], NN)

    for p in range(PARTS):
        csend[p] = proj_part(1 - core, p).astype(BF)
        core_copy(p).start()

    for n in range(D // 512):
        part = dot(kv_low[...], wcat[n * 512 : (n + 1) * 512, :], NT)
        ipart[:, :, n * 512 : (n + 1) * 512] = part.reshape(NZ, 32, 512)

    def z_copy(direction, k, half):
        return remote(
            zs.at[direction, k, half], zr.at[direction, k, half],
            z_ss.at[direction, k, half], z_rs.at[direction, k, half],
            z_mate(1 - 2 * direction),
        )

    def z_send(direction, k, half, add):
        t = lax.rem(hd + 4 - k, NZ) if direction == 0 else lax.rem(hd + 4 + k, NZ)
        term = ipart[t, :, half * HALF : (half + 1) * HALF]
        if add:
            z_copy(direction, k - 1, half).wait_recv()
            term = term + zr[direction, k - 1, half].astype(F32)
        zs[direction, k, half] = term.astype(BF)
        z_copy(direction, k, half).start()

    def z_step(k, half, add=True):
        z_send(0, k, half, add)
        z_send(1, k, 1 - half, add)

    z_step(0, 0, False)
    z_step(1, 1, False)

    def index(axis):
        return yi if axis else x

    def mate(axis, d):
        if axis:
            return y_mate(lax.rem(yi + d, NX))
        return x_mate(lax.rem(x + d, NX))

    def st1_copy(p, d):
        a = p % 2
        return remote(
            s1.at[p, lax.rem(index(a) + d, NX)], r1.at[p, d - 1],
            st1_ss.at[p, d - 1], st1_rs.at[p, d - 1], mate(a, d),
        )

    def st2_copy(p, d, arrived=False):
        a = 1 - p % 2
        own = index(a)
        slot = lax.rem(own - d + NX, NX) if arrived else own
        return remote(
            r2.at[p, own], r2.at[p, slot], st2_ss.at[p, d - 1], st2_rs.at[p, d - 1], mate(a, d)
        )

    def ag_copy(p, d, arrived=False):
        own = index(p % 2)
        ref = gfull.at[core, p, lax.rem(own - d + NX, NX) if arrived else own]
        return remote(ref, ref, ag_ss.at[p, d - 1], ag_rs.at[p, d - 1], mate(p % 2, d))

    def pair_copy(p, d, arrived=False):
        ref = gfull.at[1 - core if arrived else core, p, lax.rem(index(p % 2) - d + NX, NX)]
        return remote(ref, ref, p_ss.at[p, d], p_rs.at[p, d], other_core)

    for p in range(PARTS):
        h32[p] = proj_part(core, p).reshape(NX, SUB, 2 * HD)

    for p in range(PARTS):
        core_copy(p).wait_recv()
        term = h32[p] + ccr[p].astype(F32).reshape(NX, SUB, 2 * HD)
        h32[p] = term
        s1[p] = term.astype(BF)
        for d in (2, 1, 3):
            st1_copy(p, d).start()

    def stage2(p):
        term = h32[p, index(p % 2)]
        for d in (1, 3, 2):
            st1_copy(p, d).wait_recv()
            term = term + r1[p, d - 1].astype(F32)
        r2[p, index(1 - p % 2)] = term.astype(BF)
        for d in (2, 1, 3):
            st2_copy(p, d).start()

    def gather(p):
        for d in (1, 3, 2):
            st2_copy(p, d, True).wait_recv()
        term = r2[p, 0].astype(F32)
        for i in range(1, NX):
            term = term + r2[p, i].astype(F32)
        gfull[core, p, index(p % 2)] = term.astype(BF)
        for d in (2, 1, 3):
            ag_copy(p, d).start()
        pair_copy(p, 0).start()

    def hand_over(p):
        for d in (1, 3, 2):
            ag_copy(p, d, True).wait_recv()
            pair_copy(p, d).start()

    z_step(1, 0)
    stage2(0)
    stage2(1)
    z_step(2, 1)
    stage2(2)
    stage2(3)
    z_step(2, 0)
    gather(0)
    gather(1)
    z_step(3, 1)
    gather(2)
    gather(3)
    z_step(3, 0)
    hand_over(0)
    hand_over(1)

    for half in range(2):
        term = ipart[hd, :, half * HALF : (half + 1) * HALF]
        for direction in range(2):
            z_copy(direction, 3, half).wait_recv()
            term = term + zr[direction, 3, half].astype(F32)
        ig_out[:, half * HALF : (half + 1) * HALF] = term.astype(BF)
    ig_copy = pltpu.make_async_copy(ig_out, ig_hbm, out_sem.at[1])
    ig_copy.start()

    hand_over(2)
    hand_over(3)

    for p in range(PARTS):
        for d in range(NX):
            pair_copy(p, d, True).wait_recv()
    gp_copy = pltpu.make_async_copy(gfull, gp_hbm, out_sem.at[2])
    gp_copy.start()

    for d in range(1, NS):

        @pl.when(sq + d < NS)
        def _():
            kv_copy(sq, seq_mate(sq + d), d - 1).wait_send()

        @pl.when(d <= sq)
        def _():
            g_copy(d).wait_send()

    for direction in range(2):
        for n in range(6):
            li_copy(direction, n).wait_send()
        for k in range(4):
            for half in range(2):
                if k > 0 or half == direction:
                    z_copy(direction, k, half).wait_send()
    for p in range(PARTS):
        core_copy(p).wait_send()
        for d in range(1, NX):
            st1_copy(p, d).wait_send()
            st2_copy(p, d).wait_send()
            ag_copy(p, d).wait_send()
        for d in range(NX):
            pair_copy(p, d).wait_send()
    qg_copy.wait()
    ig_copy.wait()
    gp_copy.wait()


def finish(qg_in, ig_in, gp_in, qg_ref, ig_ref, gk_ref, gv_ref, low, key, value, sem_in, sem_key, sem_value, sem):
    copies = [
        pltpu.make_async_copy(qg_in, qg_ref, sem.at[0]),
        pltpu.make_async_copy(ig_in, ig_ref, sem.at[1]),
    ]
    step = D // PIECES
    loads = []
    for n in range(PIECES):
        loads.append(pltpu.make_async_copy(gp_in.at[pl.ds(n * step, step), :], low.at[n], sem_in.at[n]))
        loads[-1].start()
    for c in copies:
        c.start()
    for n in range(PIECES):
        rows = pl.ds(n * step, step)
        loads[n].wait()
        key[n] = low[n, :, 0:HD].astype(F32)
        copies.append(pltpu.make_async_copy(key.at[n], gk_ref.at[rows, :], sem_key.at[n]))
        copies[-1].start()
        value[n] = low[n, :, HD:].astype(F32)
        copies.append(pltpu.make_async_copy(value.at[n], gv_ref.at[rows, :], sem_value.at[n]))
        copies[-1].start()
    for c in copies:
        c.wait()


def shards(queries, key_cache, value_cache, out_grad, doc_ids, layer_input, key_proj, value_proj):
    hbm = pl.BlockSpec(memory_space=pl.ANY)
    dma = pltpu.SemaphoreType.DMA
    scratch = [
        pltpu.VMEM((GROUP, ROWS, HD), BF),
        pltpu.VMEM((GROUP, ROWS, HD), BF),
        pltpu.VMEM((1, ROWS), jnp.int32),
        pltpu.VMEM((NS, 2 * ROWS + 16, HD), BF),
        pltpu.VMEM((NZ, 32, D), BF),
        pltpu.VMEM((D, ROWS), BF),
        pltpu.VMEM((D, 2 * HD), BF),
        pltpu.VMEM((NS, GROUP, ROWS, ROWS), F32),
        pltpu.VMEM((NS, GROUP, ROWS, ROWS), F32),
        pltpu.VMEM((NS, 8, ROWS), F32),
        pltpu.VMEM((NS, 8, ROWS), F32),
        pltpu.VMEM((NS, 8, ROWS), F32),
        pltpu.VMEM((NS, 8, ROWS), F32),
        pltpu.VMEM((GROUP, HD, ROWS), F32),
        pltpu.VMEM((NS, ROWS, 2 * HD), BF),
        pltpu.VMEM((NS - 1, ROWS, 2 * HD), BF),
        pltpu.VMEM((ROWS, 2 * HD), F32),
        pltpu.VMEM((ROWS, 2 * HD), BF),
        pltpu.VMEM((NZ, 32, D), F32),
        pltpu.VMEM((2, 4, 2, 32, HALF), BF),
        pltpu.VMEM((2, 4, 2, 32, HALF), BF),
        pltpu.VMEM((32, D), BF),
        pltpu.VMEM((PARTS, PART, 2 * HD), BF),
        pltpu.VMEM((PARTS, PART, 2 * HD), BF),
        pltpu.VMEM((PARTS, NX, SUB, 2 * HD), F32),
        pltpu.VMEM((PARTS, NX, SUB, 2 * HD), BF),
        pltpu.VMEM((PARTS, NX - 1, SUB, 2 * HD), BF),
        pltpu.VMEM((PARTS, NX, SUB, 2 * HD), BF),
        pltpu.VMEM((2, PARTS, NX, SUB, 2 * HD), BF),
        pltpu.VMEM((ROWS, GROUP * HD), BF),
        dma((12,)),
        dma((NS - 1,)),
        dma((NS,)),
        dma((2, 6)),
        dma((2, 6)),
        dma((NS - 1,)),
        dma((NS - 1,)),
        dma((2, 4, 2)),
        dma((2, 4, 2)),
        dma((PARTS,)),
        dma((PARTS,)),
        dma((PARTS, 3)),
        dma((PARTS, 3)),
        dma((PARTS, 3)),
        dma((PARTS, 3)),
        dma((PARTS, 3)),
        dma((PARTS, 3)),
        dma((PARTS, 4)),
        dma((PARTS, 4)),
        dma((3,)),
    ]
    qg, ig, gp = pl.pallas_call(
        kernel,
        out_shape=(
            jax.ShapeDtypeStruct((ROWS, GROUP * HD), BF),
            jax.ShapeDtypeStruct((32, D), BF),
            jax.ShapeDtypeStruct((2, PARTS, NX, SUB, 2 * HD), BF),
        ),
        in_specs=[hbm] * 8,
        out_specs=(hbm, hbm, hbm),
        scratch_shapes=scratch,
        compiler_params=pltpu.CompilerParams(
            collective_id=0, has_side_effects=True, vmem_limit_bytes=56 * 1024 * 1024
        ),
        cost_estimate=pl.CostEstimate(
            flops=3 * 10**9, bytes_accessed=8 * 10**6, transcendentals=2 * 10**6
        ),
    )(
        queries[0], key_cache[0], value_cache[0], out_grad[0], doc_ids, layer_input[0],
        key_proj, value_proj,
    )
    step = D // PIECES
    qg, ig, gk, gv = pl.pallas_call(
        finish,
        out_shape=(
            jax.ShapeDtypeStruct((ROWS, GROUP * HD), BF),
            jax.ShapeDtypeStruct((32, D), BF),
            jax.ShapeDtypeStruct((D, HD), F32),
            jax.ShapeDtypeStruct((D, HD), F32),
        ),
        in_specs=[hbm] * 3,
        out_specs=(hbm,) * 4,
        scratch_shapes=[
            pltpu.VMEM((PIECES, step, 2 * HD), BF),
            pltpu.VMEM((PIECES, step, HD), F32),
            pltpu.VMEM((PIECES, step, HD), F32),
            dma((PIECES,)),
            dma((PIECES,)),
            dma((PIECES,)),
            dma((2,)),
        ],
        compiler_params=pltpu.CompilerParams(vmem_limit_bytes=60 * 1024 * 1024),
        cost_estimate=pl.CostEstimate(flops=0, bytes_accessed=6 * 10**6, transcendentals=0),
    )(qg, ig, gp.reshape(D, 2 * HD))
    return qg[None], ig[None], gk, gv


def solution(mesh):
    return jax.shard_map(
        shards,
        mesh=mesh,
        in_specs=(
            P("dp", "seq", "head"),
            P("dp", "seq", "head"),
            P("dp", "seq", "head"),
            P("dp", "seq", "head"),
            P("dp", "seq"),
            P("dp", ("seq", "head"), None),
            P(None, "head"),
            P(None, "head"),
        ),
        out_specs=(
            P("dp", "seq", "head"),
            P("dp", ("seq", "head"), None),
            P(None, "head"),
            P(None, "head"),
        ),
        check_vma=False,
    )
```

time: 75 us -> 80.3 us (1.071)
  Pallas kernels: 69.6 us -> 79.5 us
  other arithmetic: 3.28 us -> 0 us
  local copies, waits for them, and re-layouts: 1.36 us -> 0 us
    pallas_call x0 -> x1, Pallas kernels: none -> 13.2 us  [shards(): pl.pallas_call(finish, out_shape=(jax.ShapeDtypeStruct((ROWS, GROUP * HD)...]
    convert_element_type x1 -> x0, other arithmetic: 3.28 us -> none  [shards(): grads[:, HD:].astype(F32)]
    pallas_call x1, Pallas kernels: 69.6 us -> 66.4 us  [shards(): pl.pallas_call(kernel, out_shape=(jax.ShapeDtypeStruct((ROWS, GROUP * HD)...]
    unnamed x6 -> x0, local copies, waits for them, and re-layouts: 1.36 us -> none
where the time goes in v2:
time: 80.3 us; the launch traced here: 80.2 us
  Pallas kernels  79.5 us (99%)
    pallas_call x1, Pallas kernels, shards(): pl.pallas_call(kernel, out_shape=(jax.ShapeDtypeStruct((ROWS, GROUP * HD)...  66.4 us
    pallas_call x1, Pallas kernels, shards(): pl.pallas_call(finish, out_shape=(jax.ShapeDtypeStruct((ROWS, GROUP * HD)...  13.2 us

profile of v2, /device:TPU:1, one launch (start us, length us, event | category | flops | bytes accessed | tf_op | source)
XLA Modules:
  0.0 80.2 jit_solution(11239488581451336394)
XLA Ops:
  0.6 66.4 %shard_map.111 = (bf16[256,384]{1,0:T(8,128)(2,1)}, bf16[32,3072]{1,0:T(8,128)(2,1)}, bf16[2,4,4,96,256]{4,3,2,1,0:T(8,128)(2,1)}) custom-call(bf16[256,384]{1,0:T(8,128)(2,1)} %bitcast.9, bf16[256,128]{1,0:T(8,128)(2,1)} %bitcast.14, bf16[256,128]{1,0:T(8,128)(2,1)} %bitcast.15, bf16[256,384]{1,0:T(8,128)(2,1)} %bitcast.10, s32[1,256]{1,0:T(1,128)} %docs_hbm.1, ...), custom_call_target="tpu_custom_call" | custom-call | flops 3000000000 | bytes 8000000 | tf_op jit(solution)/shard_map/pallas_call | solution.py:514
  67.0 13.2 %shard_map.112 = (bf16[256,384]{1,0:T(8,128)(2,1)}, bf16[32,3072]{1,0:T(8,128)(2,1)}, f32[3072,128]{1,0:T(8,128)}, f32[3072,128]{1,0:T(8,128)}) custom-call(bf16[256,384]{1,0:T(8,128)(2,1)} %get-tuple-element.11.qg_in, bf16[32,3072]{1,0:T(8,128)(2,1)} %get-tuple-element.12.ig_in, bf16[3072,256]{1,0:T(8,128)(2,1)} %bitcast.8), custom_call_target="tpu_custom_call" | custom-call | bytes 6000000 | tf_op jit(solution)/shard_map/pallas_call | solution.py:535

commit v3 on v2

--- a/solution.py
+++ b/solution.py
@@ -38,12 +38,12 @@
     qg_hbm, ig_hbm, gp_hbm,
     q_v, do_v, docs_ref, kvbuf, li_buf, li_t, wcat,
     p_buf, dp_buf, m_buf, l_buf, a_buf, f_buf, dq_t,
-    gsend, grecv, acc, kv_low,
+    gsend, grecv, crecv, xsend, xrecv, acc, kv_low,
     ipart, zs, zr, ig_out,
     csend, ccr, h32, s1, r1, r2, gfull, qg_out,
-    loc, kv_ss, kv_rs, li_ss, li_rs, g_ss, g_rs,
+    loc, kv_ss, kv_rs, li_ss, li_rs, g_ss, g_rs, c_ss, c_rs, x_ss, x_rs,
     z_ss, z_rs, core_ss, core_rs, st1_ss, st1_rs, st2_ss, st2_rs,
-    ag_ss, ag_rs, p_ss, p_rs, out_sem,
+    ag_ss, ag_rs, p_ss, p_rs, out_sem, gp_sem,
 ):
     dp = lax.axis_index("dp")
     sq = lax.axis_index("seq")
@@ -54,15 +54,15 @@
     x = lax.rem(sq, NX)
     yi = y_hi * 2 + y_lo
 
-    def seq_mate(idx):
-        return (dp, idx, hd)
-
     def x_mate(idx):
         return (dp, y_hi * NX + idx, hd)
 
     def y_mate(idx):
         return (lax.rem(idx, 2) * 2 + core, lax.div(idx, 2) * NX + x, hd)
 
+    other_half = (dp, (1 - y_hi) * NX + x, hd)
+    far_x = lax.rem(x + 2, NX)
+    far_mate = (dp, (1 - y_hi) * NX + far_x, hd)
     other_core = (y_lo * 2 + 1 - core, sq, hd)
 
     def z_mate(d):
@@ -75,9 +75,9 @@
         )
 
     barrier = pltpu.get_barrier_semaphore()
-    partners = [seq_mate(lax.rem(sq + d, NS)) for d in range(1, NS)]
-    partners += [y_mate(lax.rem(yi + d, NX)) for d in (1, 3)]
-    partners += [other_core, z_mate(1), z_mate(-1), z_mate(2), z_mate(-2)]
+    partners = [x_mate(lax.rem(x + d, NX)) for d in range(1, NX)]
+    partners += [y_mate(lax.rem(yi + d, NX)) for d in range(1, NX)]
+    partners += [far_mate, other_core, z_mate(1), z_mate(-1)]
     for dev in partners:
         pl.semaphore_signal(barrier, inc=1, device_id=dev, device_id_type=pl.DeviceIdType.MESH)
 
@@ -111,41 +111,6 @@
     kvbuf[sq, pl.ds(2 * ROWS, 16), :] = doc_tile.astype(BF)
     for c in loads[1:4]:
         c.wait()
-    pl.semaphore_wait(barrier, len(partners))
-
-    def kv_copy(block, dev, s):
-        return remote(kvbuf.at[block], kvbuf.at[block], kv_ss.at[s], kv_rs.at[block], dev)
-
-    def kv_arrived(block):
-        return kv_copy(block, seq_mate(lax.rem(sq + 1, NS)), 0)
-
-    for d in range(NS - 1, 0, -1):
-
-        @pl.when(sq + d < NS)
-        def _():
-            kv_copy(sq, seq_mate(sq + d), d - 1).start()
-
-    li_moves = ((1, 0, (0, 32)), (2, 0, (0, 16)), (1, 1, (16, 16)), (2, 1, (0, 16)), (1, 2, (16, 16)), None)
-
-    def li_copy(direction, n, arrived=False):
-        hops, away, (row, size) = li_moves[n] or (2, 2, (16 * direction, 16))
-        sign = 1 - 2 * direction
-        away = away + hops if arrived else away
-        ref = li_buf.at[lax.rem(hd - sign * away + NZ, NZ), pl.ds(row, size), :]
-        return remote(ref, ref, li_ss.at[direction, n], li_rs.at[direction, n], z_mate(sign * hops))
-
-    def li_start(*moves):
-        for n in moves:
-            for direction in range(2):
-                li_copy(direction, n).start()
-
-    def li_wait(*moves):
-        for n in moves:
-            for direction in range(2):
-                li_copy(direction, n, True).wait_recv()
-
-    li_start(0, 1)
-
     for c in loads[4:10]:
         c.wait()
 
@@ -175,6 +140,59 @@
             a_buf[b, g : g + 1, :] = jnp.sum(p * wg, axis=0, keepdims=True)
 
     score_block(sq, True)
+    pl.semaphore_wait(barrier, len(partners))
+
+    def kv_copy(block, dev, s):
+        return remote(kvbuf.at[block], kvbuf.at[block], kv_ss.at[s], kv_rs.at[block], dev)
+
+    def kv_arrived(block):
+        return kv_copy(block, other_half, 0)
+
+    @pl.when(y_hi == 0)
+    def _():
+        kv_copy(sq, other_half, 3).start()
+        kv_copy(sq, far_mate, 4).start()
+
+    for d in (2, 1, 3):
+        xt = lax.rem(x + d, NX)
+
+        @pl.when(xt > x)
+        def _():
+            kv_copy(sq, x_mate(xt), d - 1).start()
+
+    def li_copy(direction, n, arrived=False):
+        sign = 1 - 2 * direction
+        away = n // 2 + 1 if arrived else n // 2
+        half = direction if n == 6 else n % 2
+        ref = li_buf.at[lax.rem(hd - sign * away + NZ, NZ), pl.ds(16 * half, 16), :]
+        return remote(ref, ref, li_ss.at[direction, n], li_rs.at[direction, n], z_mate(sign))
+
+    def li_start(n):
+        for direction in range(2):
+            li_copy(direction, n).start()
+
+    def li_wait(n):
+        for direction in range(2):
+            li_copy(direction, n, True).wait_recv()
+
+    def li_next(n):
+        li_wait(n)
+        if n == 4:
+            li_copy(0, 6).start()
+        elif n == 5:
+            li_copy(1, 6).start()
+        else:
+            li_start(n + 2)
+
+    li_start(0)
+    li_start(1)
+    li_next(0)
+
+    @pl.when(y_hi == 1)
+    def _():
+        kv_arrived(x).wait_recv()
+        for n, d in enumerate((1, 3)):
+            kv_copy(x, x_mate(lax.rem(x + d, NX)), 5 + n).start()
 
     @pl.loop(1, NX)
     def _(d):
@@ -183,15 +201,23 @@
             kv_arrived(sq - d).wait_recv()
             score_block(sq - d, False)
 
-    li_wait(0)
-    li_start(2, 3)
+    li_next(1)
 
     @pl.when(y_hi == 1)
     def _():
-        @pl.loop(0, NX)
-        def _(d):
-            kv_arrived(NX - 1 - d).wait_recv()
-            score_block(NX - 1 - d, False)
+        score_block(x, False)
+
+    li_next(2)
+
+    @pl.when(y_hi == 1)
+    def _():
+        @pl.loop(0, NX - 1)
+        def _(n):
+            b = lax.rem(x + 2 + n + lax.div(n, 2), NX)
+            kv_arrived(b).wait_recv()
+            score_block(b, False)
+
+    li_next(3)
 
     top = jnp.max(m_buf[...], axis=0)
     factor = jnp.exp2((m_buf[...] - top[None]) * EXP_SCALE)
@@ -216,24 +242,53 @@
         gsend[b, :, HD:] = dv.astype(BF)
 
     def g_copy(d):
+        xt = lax.rem(x + d, NX)
         return remote(
-            gsend.at[sq - d], grecv.at[d - 1], g_ss.at[d - 1], g_rs.at[d - 1], seq_mate(sq - d)
+            gsend.at[y_hi * NX + xt], grecv.at[d - 1], g_ss.at[d - 1], g_rs.at[d - 1], x_mate(xt)
         )
 
-    def g_arrived(d):
-        return remote(
-            gsend.at[sq], grecv.at[d - 1], g_ss.at[d - 1], g_rs.at[d - 1], seq_mate(sq + d)
-        )
-
-    @pl.loop(0, NS - 1)
-    def _(b):
-        @pl.when(b < sq)
+    def c_copy(n):
+        xt = lax.rem(x + 1 + 2 * n, NX)
+        return remote(gsend.at[xt], crecv.at[n], c_ss.at[n], c_rs.at[n], x_mate(xt))
+
+    far_copy = remote(gsend.at[far_x], xrecv.at[0], x_ss.at[0], x_rs.at[0], far_mate)
+    cross = remote(xsend, xrecv.at[1], x_ss.at[1], x_rs.at[1], other_half)
+
+    @pl.when(y_hi == 1)
+    def _():
+        grad_block(far_x)
+        far_copy.start()
+
+        @pl.loop(0, 2)
+        def _(n):
+            grad_block(lax.rem(x + 1 + 2 * n, NX))
+            c_copy(n).start()
+
+    li_next(4)
+
+    @pl.when(y_hi == 1)
+    def _():
+        grad_block(x)
+
+    @pl.loop(1, NX)
+    def _(d):
+        xt = lax.rem(x + d, NX)
+
+        @pl.when(xt < x)
         def _():
-            grad_block(b)
-            g_copy(sq - b).start()
-
-    li_wait(1, 2)
-    li_start(4, 5)
+            grad_block(y_hi * NX + xt)
+            g_copy(d).start()
+
+    li_next(5)
+
+    @pl.when(y_hi == 1)
+    def _():
+        acc[...] = gsend[x].astype(F32)
+        for n in range(2):
+            c_copy(n).wait_recv()
+            acc[...] += crecv[n].astype(F32)
+        xsend[...] = acc[...].astype(BF)
+        cross.start()
 
     grad_block(sq)
 
@@ -245,21 +300,27 @@
     for c in loads[10:]:
         c.wait()
 
-    acc[...] = gsend[sq].astype(F32)
-
-    @pl.loop(1, NS)
-    def _(d):
-        @pl.when(sq + d < NS)
-        def _():
-            g_arrived(d).wait_recv()
-            acc[...] += grecv[d - 1].astype(F32)
-
-    kv_low[...] = acc[...].astype(BF)
-
-    li_wait(3, 4, 5)
+    li_wait(6)
     for n in range(D // 512):
         cols = li_buf[:, :, n * 512 : (n + 1) * 512].reshape(ROWS, 512)
         li_t[n * 512 : (n + 1) * 512, :] = cols.T
+
+    acc[...] = gsend[sq].astype(F32)
+
+    for d in range(1, NX):
+
+        @pl.when(lax.rem(x - d + NX, NX) > x)
+        def _():
+            g_copy(d).wait_recv()
+            acc[...] += grecv[d - 1].astype(F32)
+
+    @pl.when(y_hi == 0)
+    def _():
+        far_copy.wait_recv()
+        cross.wait_recv()
+        acc[...] += xrecv[0].astype(F32) + xrecv[1].astype(F32)
+
+    kv_low[...] = acc[...].astype(BF)
 
     def core_copy(p):
         return remote(csend.at[p], ccr.at[p], core_ss.at[p], core_rs.at[p], other_core)
@@ -392,27 +453,48 @@
     ig_copy = pltpu.make_async_copy(ig_out, ig_hbm, out_sem.at[1])
     ig_copy.start()
 
-    hand_over(2)
-    hand_over(3)
-
-    for p in range(PARTS):
+    def gp_copy(c, p):
+        return pltpu.make_async_copy(gfull.at[c, p], gp_hbm.at[c, p], gp_sem.at[c, p])
+
+    def part_done(p):
         for d in range(NX):
             pair_copy(p, d, True).wait_recv()
-    gp_copy = pltpu.make_async_copy(gfull, gp_hbm, out_sem.at[2])
-    gp_copy.start()
-
-    for d in range(1, NS):
-
-        @pl.when(sq + d < NS)
+        for c in range(2):
+            gp_copy(c, p).start()
+
+    hand_over(2)
+    part_done(0)
+    part_done(1)
+    hand_over(3)
+    part_done(2)
+    part_done(3)
+
+    for d in range(1, NX):
+        xt = lax.rem(x + d, NX)
+
+        @pl.when(xt > x)
         def _():
-            kv_copy(sq, seq_mate(sq + d), d - 1).wait_send()
-
-        @pl.when(d <= sq)
+            kv_copy(sq, x_mate(xt), d - 1).wait_send()
+
+        @pl.when(xt < x)
         def _():
             g_copy(d).wait_send()
 
+    @pl.when(y_hi == 0)
+    def _():
+        kv_copy(sq, other_half, 3).wait_send()
+        kv_copy(sq, far_mate, 4).wait_send()
+
+    @pl.when(y_hi == 1)
+    def _():
+        for n, d in enumerate((1, 3)):
+            kv_copy(x, x_mate(lax.rem(x + d, NX)), 5 + n).wait_send()
+            c_copy(n).wait_send()
+        far_copy.wait_send()
+        cross.wait_send()
+
     for direction in range(2):
-        for n in range(6):
+        for n in range(7):
             li_copy(direction, n).wait_send()
         for k in range(4):
             for half in range(2):
@@ -428,21 +510,25 @@
             pair_copy(p, d).wait_send()
     qg_copy.wait()
     ig_copy.wait()
-    gp_copy.wait()
-
-
-def finish(qg_in, ig_in, gp_in, qg_ref, ig_ref, gk_ref, gv_ref, low, key, value, sem_in, sem_key, sem_value, sem):
-    copies = [
-        pltpu.make_async_copy(qg_in, qg_ref, sem.at[0]),
-        pltpu.make_async_copy(ig_in, ig_ref, sem.at[1]),
+    for p in range(PARTS):
+        for c in range(2):
+            gp_copy(c, p).wait()
+
+
+def finish(
+    qg_in, ig_in, gp_in, qg_ref, ig_ref, gk_ref, gv_ref,
+    low, key, value, qg_v, ig_v, sem_in, sem_key, sem_value, sem,
+):
+    step = D // PIECES
+    loads = [
+        pltpu.make_async_copy(gp_in.at[pl.ds(n * step, step), :], low.at[n], sem_in.at[n])
+        for n in range(PIECES)
     ]
-    step = D // PIECES
-    loads = []
-    for n in range(PIECES):
-        loads.append(pltpu.make_async_copy(gp_in.at[pl.ds(n * step, step), :], low.at[n], sem_in.at[n]))
-        loads[-1].start()
-    for c in copies:
+    loads.append(pltpu.make_async_copy(qg_in, qg_v, sem.at[0]))
+    loads.append(pltpu.make_async_copy(ig_in, ig_v, sem.at[1]))
+    for c in loads:
         c.start()
+    copies = []
     for n in range(PIECES):
         rows = pl.ds(n * step, step)
         loads[n].wait()
@@ -452,6 +538,12 @@
         value[n] = low[n, :, HD:].astype(F32)
         copies.append(pltpu.make_async_copy(value.at[n], gv_ref.at[rows, :], sem_value.at[n]))
         copies[-1].start()
+    loads[PIECES].wait()
+    copies.append(pltpu.make_async_copy(qg_v, qg_ref, sem.at[2]))
+    copies[-1].start()
+    loads[PIECES + 1].wait()
+    copies.append(pltpu.make_async_copy(ig_v, ig_ref, sem.at[3]))
+    copies[-1].start()
     for c in copies:
         c.wait()
 
@@ -475,7 +567,10 @@
         pltpu.VMEM((NS, 8, ROWS), F32),
         pltpu.VMEM((GROUP, HD, ROWS), F32),
         pltpu.VMEM((NS, ROWS, 2 * HD), BF),
-        pltpu.VMEM((NS - 1, ROWS, 2 * HD), BF),
+        pltpu.VMEM((NX - 1, ROWS, 2 * HD), BF),
+        pltpu.VMEM((2, ROWS, 2 * HD), BF),
+        pltpu.VMEM((ROWS, 2 * HD), BF),
+        pltpu.VMEM((2, ROWS, 2 * HD), BF),
         pltpu.VMEM((ROWS, 2 * HD), F32),
         pltpu.VMEM((ROWS, 2 * HD), BF),
         pltpu.VMEM((NZ, 32, D), F32),
@@ -491,12 +586,16 @@
         pltpu.VMEM((2, PARTS, NX, SUB, 2 * HD), BF),
         pltpu.VMEM((ROWS, GROUP * HD), BF),
         dma((12,)),
-        dma((NS - 1,)),
+        dma((7,)),
         dma((NS,)),
-        dma((2, 6)),
-        dma((2, 6)),
-        dma((NS - 1,)),
-        dma((NS - 1,)),
+        dma((2, 7)),
+        dma((2, 7)),
+        dma((NX - 1,)),
+        dma((NX - 1,)),
+        dma((2,)),
+        dma((2,)),
+        dma((2,)),
+        dma((2,)),
         dma((2, 4, 2)),
         dma((2, 4, 2)),
         dma((PARTS,)),
@@ -509,7 +608,8 @@
         dma((PARTS, 3)),
         dma((PARTS, 4)),
         dma((PARTS, 4)),
-        dma((3,)),
+        dma((2,)),
+        dma((2, PARTS)),
     ]
     qg, ig, gp = pl.pallas_call(
         kernel,
@@ -546,10 +646,12 @@
             pltpu.VMEM((PIECES, step, 2 * HD), BF),
             pltpu.VMEM((PIECES, step, HD), F32),
             pltpu.VMEM((PIECES, step, HD), F32),
+            pltpu.VMEM((ROWS, GROUP * HD), BF),
+            pltpu.VMEM((32, D), BF),
             dma((PIECES,)),
             dma((PIECES,)),
             dma((PIECES,)),
-            dma((2,)),
+            dma((4,)),
         ],
         compiler_params=pltpu.CompilerParams(vmem_limit_bytes=60 * 1024 * 1024),
         cost_estimate=pl.CostEstimate(flops=0, bytes_accessed=6 * 10**6, transcendentals=0),

time: 80.3 us -> 67.3 us (0.84)
  Pallas kernels: 79.5 us -> 66.5 us
    pallas_call x1, Pallas kernels: 13.2 us -> 2.94 us  [shards(): pl.pallas_call(finish, out_shape=(jax.ShapeDtypeStruct((ROWS, GROUP * HD)...]
    pallas_call x1, Pallas kernels: 66.4 us -> 63.6 us  [shards(): pl.pallas_call(kernel, out_shape=(jax.ShapeDtypeStruct((ROWS, GROUP * HD)...]
where the time goes in v3:
time: 67.3 us; the launch traced here: 67.2 us
  Pallas kernels  66.5 us (99%)
    pallas_call x1, Pallas kernels, shards(): pl.pallas_call(kernel, out_shape=(jax.ShapeDtypeStruct((ROWS, GROUP * HD)...  63.6 us
    pallas_call x1, Pallas kernels, shards(): pl.pallas_call(finish, out_shape=(jax.ShapeDtypeStruct((ROWS, GROUP * HD)...  2.94 us

profile of v3, /device:TPU:1, one launch (start us, length us, event | category | flops | bytes accessed | tf_op | source)
XLA Modules:
  0.0 67.2 jit_solution(1678304475861099823)
XLA Ops:
  0.6 63.6 %shard_map.111 = (bf16[256,384]{1,0:T(8,128)(2,1)}, bf16[32,3072]{1,0:T(8,128)(2,1)}, bf16[2,4,4,96,256]{4,3,2,1,0:T(8,128)(2,1)}) custom-call(bf16[256,384]{1,0:T(8,128)(2,1)} %bitcast.9, bf16[256,128]{1,0:T(8,128)(2,1)} %bitcast.14, bf16[256,128]{1,0:T(8,128)(2,1)} %bitcast.15, bf16[256,384]{1,0:T(8,128)(2,1)} %bitcast.10, s32[1,256]{1,0:T(1,128)} %docs_hbm.1, ...), custom_call_target="tpu_custom_call" | custom-call | flops 3000000000 | bytes 8000000 | tf_op jit(solution)/shard_map/pallas_call | solution.py:614
  64.2 2.9 %shard_map.112 = (bf16[256,384]{1,0:T(8,128)(2,1)}, bf16[32,3072]{1,0:T(8,128)(2,1)}, f32[3072,128]{1,0:T(8,128)}, f32[3072,128]{1,0:T(8,128)}) custom-call(bf16[256,384]{1,0:T(8,128)(2,1)} %get-tuple-element.11.qg_in, bf16[32,3072]{1,0:T(8,128)(2,1)} %get-tuple-element.12.ig_in, bf16[3072,256]{1,0:T(8,128)(2,1)} %bitcast.8), custom_call_target="tpu_custom_call" | custom-call | bytes 6000000 | tf_op jit(solution)/shard_map/pallas_call | solution.py:635

commit v4 on v3

--- a/solution.py
+++ b/solution.py
@@ -38,10 +38,10 @@
     qg_hbm, ig_hbm, gp_hbm,
     q_v, do_v, docs_ref, kvbuf, li_buf, li_t, wcat,
     p_buf, dp_buf, m_buf, l_buf, a_buf, f_buf, dq_t,
-    gsend, grecv, crecv, xsend, xrecv, acc, kv_low,
+    gsend, grecv, crecv, xsend, xrecv, frecv, acc, kv_low,
     ipart, zs, zr, ig_out,
     csend, ccr, h32, s1, r1, r2, gfull, qg_out,
-    loc, kv_ss, kv_rs, li_ss, li_rs, g_ss, g_rs, c_ss, c_rs, x_ss, x_rs,
+    loc, kv_ss, kv_rs, kv_ps, kv_pr, li_ss, li_rs, g_ss, g_rs, c_ss, c_rs, x_ss, x_rs,
     z_ss, z_rs, core_ss, core_rs, st1_ss, st1_rs, st2_ss, st2_rs,
     ag_ss, ag_rs, p_ss, p_rs, out_sem, gp_sem,
 ):
@@ -148,10 +148,15 @@
     def kv_arrived(block):
         return kv_copy(block, other_half, 0)
 
+    def kv_part(block, part, dev, s):
+        ref = kvbuf.at[block, pl.ds(part * ROWS, ROWS + 16 * part), :]
+        return remote(ref, ref, kv_ps.at[s], kv_pr.at[block, part], dev)
+
     @pl.when(y_hi == 0)
     def _():
-        kv_copy(sq, other_half, 3).start()
-        kv_copy(sq, far_mate, 4).start()
+        for part in range(2):
+            kv_part(x, part, other_half, part).start()
+        kv_copy(sq, far_mate, 3).start()
 
     for d in (2, 1, 3):
         xt = lax.rem(x + d, NX)
@@ -190,9 +195,10 @@
 
     @pl.when(y_hi == 1)
     def _():
-        kv_arrived(x).wait_recv()
-        for n, d in enumerate((1, 3)):
-            kv_copy(x, x_mate(lax.rem(x + d, NX)), 5 + n).start()
+        for part in range(2):
+            kv_part(x, part, other_half, 0).wait_recv()
+            for n, d in enumerate((1, 3)):
+                kv_part(x, part, x_mate(lax.rem(x + d, NX)), 2 + 2 * part + n).start()
 
     @pl.loop(1, NX)
     def _(d):
@@ -211,10 +217,14 @@
 
     @pl.when(y_hi == 1)
     def _():
-        @pl.loop(0, NX - 1)
+        kv_arrived(far_x).wait_recv()
+        score_block(far_x, False)
+
+        @pl.loop(0, 2)
         def _(n):
-            b = lax.rem(x + 2 + n + lax.div(n, 2), NX)
-            kv_arrived(b).wait_recv()
+            b = lax.rem(x + 1 + 2 * n, NX)
+            for part in range(2):
+                kv_part(b, part, other_half, 0).wait_recv()
             score_block(b, False)
 
     li_next(3)
@@ -247,12 +257,20 @@
             gsend.at[y_hi * NX + xt], grecv.at[d - 1], g_ss.at[d - 1], g_rs.at[d - 1], x_mate(xt)
         )
 
-    def c_copy(n):
+    def columns(part):
+        return pl.ds(part * HD, HD)
+
+    def c_copy(n, part):
         xt = lax.rem(x + 1 + 2 * n, NX)
-        return remote(gsend.at[xt], crecv.at[n], c_ss.at[n], c_rs.at[n], x_mate(xt))
-
-    far_copy = remote(gsend.at[far_x], xrecv.at[0], x_ss.at[0], x_rs.at[0], far_mate)
-    cross = remote(xsend, xrecv.at[1], x_ss.at[1], x_rs.at[1], other_half)
+        return remote(
+            gsend.at[xt, :, columns(part)], crecv.at[n, part],
+            c_ss.at[n, part], c_rs.at[n, part], x_mate(xt),
+        )
+
+    far_copy = remote(gsend.at[far_x], frecv, x_ss.at[2], x_rs.at[2], far_mate)
+
+    def cross(part):
+        return remote(xsend.at[part], xrecv.at[part], x_ss.at[part], x_rs.at[part], other_half)
 
     @pl.when(y_hi == 1)
     def _():
@@ -262,7 +280,8 @@
         @pl.loop(0, 2)
         def _(n):
             grad_block(lax.rem(x + 1 + 2 * n, NX))
-            c_copy(n).start()
+            for part in range(2):
+                c_copy(n, part).start()
 
     li_next(4)
 
@@ -283,12 +302,13 @@
 
     @pl.when(y_hi == 1)
     def _():
-        acc[...] = gsend[x].astype(F32)
-        for n in range(2):
-            c_copy(n).wait_recv()
-            acc[...] += crecv[n].astype(F32)
-        xsend[...] = acc[...].astype(BF)
-        cross.start()
+        for part in range(2):
+            term = gsend[x, :, columns(part)].astype(F32)
+            for n in range(2):
+                c_copy(n, part).wait_recv()
+                term = term + crecv[n, part].astype(F32)
+            xsend[part] = term.astype(BF)
+            cross(part).start()
 
     grad_block(sq)
 
@@ -317,8 +337,10 @@
     @pl.when(y_hi == 0)
     def _():
         far_copy.wait_recv()
-        cross.wait_recv()
-        acc[...] += xrecv[0].astype(F32) + xrecv[1].astype(F32)
+        acc[...] += frecv[...].astype(F32)
+        for part in range(2):
+            cross(part).wait_recv()
+            acc[:, columns(part)] += xrecv[part].astype(F32)
 
     kv_low[...] = acc[...].astype(BF)
 
@@ -482,16 +504,19 @@
 
     @pl.when(y_hi == 0)
     def _():
-        kv_copy(sq, other_half, 3).wait_send()
-        kv_copy(sq, far_mate, 4).wait_send()
+        for part in range(2):
+            kv_part(x, part, other_half, part).wait_send()
+        kv_copy(sq, far_mate, 3).wait_send()
 
     @pl.when(y_hi == 1)
     def _():
         for n, d in enumerate((1, 3)):
-            kv_copy(x, x_mate(lax.rem(x + d, NX)), 5 + n).wait_send()
-            c_copy(n).wait_send()
+            for part in range(2):
+                kv_part(x, part, x_mate(lax.rem(x + d, NX)), 2 + 2 * part + n).wait_send()
+                c_copy(n, part).wait_send()
         far_copy.wait_send()
-        cross.wait_send()
+        for part in range(2):
+            cross(part).wait_send()
 
     for direction in range(2):
         for n in range(7):
@@ -568,9 +593,10 @@
         pltpu.VMEM((GROUP, HD, ROWS), F32),
         pltpu.VMEM((NS, ROWS, 2 * HD), BF),
         pltpu.VMEM((NX - 1, ROWS, 2 * HD), BF),
-        pltpu.VMEM((2, ROWS, 2 * HD), BF),
+        pltpu.VMEM((2, 2, ROWS, HD), BF),
+        pltpu.VMEM((2, ROWS, HD), BF),
+        pltpu.VMEM((2, ROWS, HD), BF),
         pltpu.VMEM((ROWS, 2 * HD), BF),
-        pltpu.VMEM((2, ROWS, 2 * HD), BF),
         pltpu.VMEM((ROWS, 2 * HD), F32),
         pltpu.VMEM((ROWS, 2 * HD), BF),
         pltpu.VMEM((NZ, 32, D), F32),
@@ -586,16 +612,18 @@
         pltpu.VMEM((2, PARTS, NX, SUB, 2 * HD), BF),
         pltpu.VMEM((ROWS, GROUP * HD), BF),
         dma((12,)),
-        dma((7,)),
+        dma((NX,)),
         dma((NS,)),
+        dma((6,)),
+        dma((NX, 2)),
         dma((2, 7)),
         dma((2, 7)),
         dma((NX - 1,)),
         dma((NX - 1,)),
-        dma((2,)),
-        dma((2,)),
-        dma((2,)),
-        dma((2,)),
+        dma((2, 2)),
+        dma((2, 2)),
+        dma((3,)),
+        dma((3,)),
         dma((2, 4, 2)),
         dma((2, 4, 2)),
         dma((PARTS,)),

time: 67.3 us -> 65.5 us (0.973)
  Pallas kernels: 66.5 us -> 64.7 us
    pallas_call x1, Pallas kernels: 63.6 us -> 61.8 us  [shards(): pl.pallas_call(kernel, out_shape=(jax.ShapeDtypeStruct((ROWS, GROUP * HD)...]
where the time goes in v4:
time: 65.5 us; the launch traced here: 65.4 us
  Pallas kernels  64.7 us (99%)
    pallas_call x1, Pallas kernels, shards(): pl.pallas_call(kernel, out_shape=(jax.ShapeDtypeStruct((ROWS, GROUP * HD)...  61.8 us
    pallas_call x1, Pallas kernels, shards(): pl.pallas_call(finish, out_shape=(jax.ShapeDtypeStruct((ROWS, GROUP * HD)...  2.94 us

profile of v4, /device:TPU:1, one launch (start us, length us, event | category | flops | bytes accessed | tf_op | source)
XLA Modules:
  0.0 65.4 jit_solution(5988501891477231149)
XLA Ops:
  0.6 61.8 %shard_map.111 = (bf16[256,384]{1,0:T(8,128)(2,1)}, bf16[32,3072]{1,0:T(8,128)(2,1)}, bf16[2,4,4,96,256]{4,3,2,1,0:T(8,128)(2,1)}) custom-call(bf16[256,384]{1,0:T(8,128)(2,1)} %bitcast.9, bf16[256,128]{1,0:T(8,128)(2,1)} %bitcast.14, bf16[256,128]{1,0:T(8,128)(2,1)} %bitcast.15, bf16[256,384]{1,0:T(8,128)(2,1)} %bitcast.10, s32[1,256]{1,0:T(1,128)} %docs_hbm.1, ...), custom_call_target="tpu_custom_call" | custom-call | flops 3000000000 | bytes 8000000 | tf_op jit(solution)/shard_map/pallas_call | solution.py:642
  62.4 2.9 %shard_map.112 = (bf16[256,384]{1,0:T(8,128)(2,1)}, bf16[32,3072]{1,0:T(8,128)(2,1)}, f32[3072,128]{1,0:T(8,128)}, f32[3072,128]{1,0:T(8,128)}) custom-call(bf16[256,384]{1,0:T(8,128)(2,1)} %get-tuple-element.11.qg_in, bf16[32,3072]{1,0:T(8,128)(2,1)} %get-tuple-element.12.ig_in, bf16[3072,256]{1,0:T(8,128)(2,1)} %bitcast.8), custom_call_target="tpu_custom_call" | custom-call | bytes 6000000 | tf_op jit(solution)/shard_map/pallas_call | solution.py:663

commit v5 on v4

--- a/solution.py
+++ b/solution.py
@@ -274,14 +274,14 @@
 
     @pl.when(y_hi == 1)
     def _():
-        grad_block(far_x)
-        far_copy.start()
-
         @pl.loop(0, 2)
         def _(n):
             grad_block(lax.rem(x + 1 + 2 * n, NX))
             for part in range(2):
                 c_copy(n, part).start()
+
+        grad_block(far_x)
+        far_copy.start()
 
     li_next(4)
 
@@ -542,39 +542,30 @@
 
 def finish(
     qg_in, ig_in, gp_in, qg_ref, ig_ref, gk_ref, gv_ref,
-    low, key, value, qg_v, ig_v, sem_in, sem_key, sem_value, sem,
+    key, value, sem_key, sem_value, sem,
 ):
     step = D // PIECES
-    loads = [
-        pltpu.make_async_copy(gp_in.at[pl.ds(n * step, step), :], low.at[n], sem_in.at[n])
-        for n in range(PIECES)
+    copies = [
+        pltpu.make_async_copy(qg_in, qg_ref, sem.at[0]),
+        pltpu.make_async_copy(ig_in, ig_ref, sem.at[1]),
     ]
-    loads.append(pltpu.make_async_copy(qg_in, qg_v, sem.at[0]))
-    loads.append(pltpu.make_async_copy(ig_in, ig_v, sem.at[1]))
-    for c in loads:
+    for c in copies:
         c.start()
-    copies = []
     for n in range(PIECES):
         rows = pl.ds(n * step, step)
-        loads[n].wait()
-        key[n] = low[n, :, 0:HD].astype(F32)
+        key[n] = gp_in[rows, 0:HD].astype(F32)
         copies.append(pltpu.make_async_copy(key.at[n], gk_ref.at[rows, :], sem_key.at[n]))
         copies[-1].start()
-        value[n] = low[n, :, HD:].astype(F32)
+        value[n] = gp_in[rows, HD:].astype(F32)
         copies.append(pltpu.make_async_copy(value.at[n], gv_ref.at[rows, :], sem_value.at[n]))
         copies[-1].start()
-    loads[PIECES].wait()
-    copies.append(pltpu.make_async_copy(qg_v, qg_ref, sem.at[2]))
-    copies[-1].start()
-    loads[PIECES + 1].wait()
-    copies.append(pltpu.make_async_copy(ig_v, ig_ref, sem.at[3]))
-    copies[-1].start()
     for c in copies:
         c.wait()
 
 
 def shards(queries, key_cache, value_cache, out_grad, doc_ids, layer_input, key_proj, value_proj):
     hbm = pl.BlockSpec(memory_space=pl.ANY)
+    vmem = pl.BlockSpec(memory_space=pltpu.VMEM)
     dma = pltpu.SemaphoreType.DMA
     scratch = [
         pltpu.VMEM((GROUP, ROWS, HD), BF),
@@ -642,12 +633,12 @@
     qg, ig, gp = pl.pallas_call(
         kernel,
         out_shape=(
-            jax.ShapeDtypeStruct((ROWS, GROUP * HD), BF),
-            jax.ShapeDtypeStruct((32, D), BF),
-            jax.ShapeDtypeStruct((2, PARTS, NX, SUB, 2 * HD), BF),
+            pltpu.VMEM((ROWS, GROUP * HD), BF),
+            pltpu.VMEM((32, D), BF),
+            pltpu.VMEM((2, PARTS, NX, SUB, 2 * HD), BF),
         ),
         in_specs=[hbm] * 8,
-        out_specs=(hbm, hbm, hbm),
+        out_specs=(vmem,) * 3,
         scratch_shapes=scratch,
         compiler_params=pltpu.CompilerParams(
             collective_id=0, has_side_effects=True, vmem_limit_bytes=56 * 1024 * 1024
@@ -668,20 +659,16 @@
             jax.ShapeDtypeStruct((D, HD), F32),
             jax.ShapeDtypeStruct((D, HD), F32),
         ),
-        in_specs=[hbm] * 3,
+        in_specs=[vmem] * 3,
         out_specs=(hbm,) * 4,
         scratch_shapes=[
-            pltpu.VMEM((PIECES, step, 2 * HD), BF),
             pltpu.VMEM((PIECES, step, HD), F32),
             pltpu.VMEM((PIECES, step, HD), F32),
-            pltpu.VMEM((ROWS, GROUP * HD), BF),
-            pltpu.VMEM((32, D), BF),
             dma((PIECES,)),
             dma((PIECES,)),
-            dma((PIECES,)),
-            dma((4,)),
+            dma((2,)),
         ],
-        compiler_params=pltpu.CompilerParams(vmem_limit_bytes=60 * 1024 * 1024),
+        compiler_params=pltpu.CompilerParams(vmem_limit_bytes=24 * 1024 * 1024),
         cost_estimate=pl.CostEstimate(flops=0, bytes_accessed=6 * 10**6, transcendentals=0),
     )(qg, ig, gp.reshape(D, 2 * HD))
     return qg[None], ig[None], gk, gv

time: 65.5 us -> 65.6 us (level)
    pallas_call x1, Pallas kernels: 61.8 us -> 63 us  [shards(): pl.pallas_call(kernel, out_shape=(pltpu.VMEM((ROWS, GROUP * HD), BF), plt...]
    pallas_call x1, Pallas kernels: 2.94 us -> 1.88 us  [shards(): pl.pallas_call(finish, out_shape=(jax.ShapeDtypeStruct((ROWS, GROUP * HD)...]
where the time goes in v5:
time: 65.6 us; the launch traced here: 65.5 us
  Pallas kernels  64.9 us (99%)
    pallas_call x1, Pallas kernels, shards(): pl.pallas_call(kernel, out_shape=(pltpu.VMEM((ROWS, GROUP * HD), BF), plt...  63 us
    pallas_call x1, Pallas kernels, shards(): pl.pallas_call(finish, out_shape=(jax.ShapeDtypeStruct((ROWS, GROUP * HD)...  1.88 us

profile of v5, /device:TPU:1, one launch (start us, length us, event | category | flops | bytes accessed | tf_op | source)
XLA Modules:
  0.0 65.5 jit_solution(12017658571464736767)
XLA Ops:
  0.6 63.0 %shard_map.111 = (bf16[256,384]{1,0:T(8,128)(2,1)S(1)}, bf16[32,3072]{1,0:T(8,128)(2,1)S(1)}, bf16[2,4,4,96,256]{4,3,2,1,0:T(8,128)(2,1)S(1)}) custom-call(bf16[256,384]{1,0:T(8,128)(2,1)} %bitcast.9, bf16[256,128]{1,0:T(8,128)(2,1)} %bitcast.14, bf16[256,128]{1,0:T(8,128)(2,1)} %bitcast.15, bf16[256,384]{1,0:T(8,128)(2,1)} %bitcast.10, s32[1,256]{1,0:T(1,128)} %docs_hbm.1, ...), custom_call_target="tpu_custom_call" | custom-call | flops 3000000000 | bytes 8000000 | tf_op jit(solution)/shard_map/pallas_call | solution.py:633
  63.6 1.9 %shard_map.112 = (bf16[256,384]{1,0:T(8,128)(2,1)}, bf16[32,3072]{1,0:T(8,128)(2,1)}, f32[3072,128]{1,0:T(8,128)}, f32[3072,128]{1,0:T(8,128)}) custom-call(bf16[256,384]{1,0:T(8,128)(2,1)S(1)} %get-tuple-element.11.qg_in, bf16[32,3072]{1,0:T(8,128)(2,1)S(1)} %get-tuple-element.12.ig_in, bf16[3072,256]{1,0:T(8,128)(2,1)S(1)} %bitcast.8), custom_call_target="tpu_custom_call" | custom-call | bytes 6000000 | tf_op jit(solution)/shard_map/pallas_call | solution.py:654

commit v6 on v5

--- a/solution.py
+++ b/solution.py
@@ -35,15 +35,15 @@
 
 def kernel(
     q_hbm, k_hbm, v_hbm, do_hbm, docs_hbm, li_hbm, wk_hbm, wv_hbm,
-    qg_hbm, ig_hbm, gp_hbm,
+    qg_out, ig_out, gfull,
     q_v, do_v, docs_ref, kvbuf, li_buf, li_t, wcat,
     p_buf, dp_buf, m_buf, l_buf, a_buf, f_buf, dq_t,
     gsend, grecv, crecv, xsend, xrecv, frecv, acc, kv_low,
-    ipart, zs, zr, ig_out,
-    csend, ccr, h32, s1, r1, r2, gfull, qg_out,
+    ipart, zs, zr,
+    csend, ccr, h32, s1, r1, r2,
     loc, kv_ss, kv_rs, kv_ps, kv_pr, li_ss, li_rs, g_ss, g_rs, c_ss, c_rs, x_ss, x_rs,
     z_ss, z_rs, core_ss, core_rs, st1_ss, st1_rs, st2_ss, st2_rs,
-    ag_ss, ag_rs, p_ss, p_rs, out_sem, gp_sem,
+    ag_ss, ag_rs, p_ss, p_rs,
 ):
     dp = lax.axis_index("dp")
     sq = lax.axis_index("seq")
@@ -109,8 +109,61 @@
         jnp.broadcast_to(doc_row[:, HD:], (16, HD)),
     )
     kvbuf[sq, pl.ds(2 * ROWS, 16), :] = doc_tile.astype(BF)
-    for c in loads[1:4]:
+    for c in loads[1:3]:
         c.wait()
+    pl.semaphore_wait(barrier, len(partners))
+
+    def kv_copy(block, dev, s):
+        return remote(kvbuf.at[block], kvbuf.at[block], kv_ss.at[s], kv_rs.at[block], dev)
+
+    def kv_arrived(block):
+        return kv_copy(block, other_half, 0)
+
+    def kv_part(block, part, dev, s):
+        ref = kvbuf.at[block, pl.ds(part * ROWS, ROWS + 16 * part), :]
+        return remote(ref, ref, kv_ps.at[s], kv_pr.at[block, part], dev)
+
+    @pl.when(y_hi == 0)
+    def _():
+        for part in range(2):
+            kv_part(x, part, other_half, part).start()
+        kv_copy(sq, far_mate, 3).start()
+
+    for d in (2, 1, 3):
+        xt = lax.rem(x + d, NX)
+
+        @pl.when(xt > x)
+        def _():
+            kv_copy(sq, x_mate(xt), d - 1).start()
+
+    def li_copy(direction, n, arrived=False):
+        sign = 1 - 2 * direction
+        away = n // 2 + 1 if arrived else n // 2
+        half = direction if n == 6 else n % 2
+        ref = li_buf.at[lax.rem(hd - sign * away + NZ, NZ), pl.ds(16 * half, 16), :]
+        return remote(ref, ref, li_ss.at[direction, n], li_rs.at[direction, n], z_mate(sign))
+
+    def li_start(n):
+        for direction in range(2):
+            li_copy(direction, n).start()
+
+    def li_wait(n):
+        for direction in range(2):
+            li_copy(direction, n, True).wait_recv()
+
+    def li_next(n):
+        li_wait(n)
+        if n == 4:
+            li_copy(0, 6).start()
+        elif n == 5:
+            li_copy(1, 6).start()
+        else:
+            li_start(n + 2)
+
+    loads[3].wait()
+    li_start(0)
+    li_start(1)
+
     for c in loads[4:10]:
         c.wait()
 
@@ -140,57 +193,7 @@
             a_buf[b, g : g + 1, :] = jnp.sum(p * wg, axis=0, keepdims=True)
 
     score_block(sq, True)
-    pl.semaphore_wait(barrier, len(partners))
-
-    def kv_copy(block, dev, s):
-        return remote(kvbuf.at[block], kvbuf.at[block], kv_ss.at[s], kv_rs.at[block], dev)
-
-    def kv_arrived(block):
-        return kv_copy(block, other_half, 0)
-
-    def kv_part(block, part, dev, s):
-        ref = kvbuf.at[block, pl.ds(part * ROWS, ROWS + 16 * part), :]
-        return remote(ref, ref, kv_ps.at[s], kv_pr.at[block, part], dev)
-
-    @pl.when(y_hi == 0)
-    def _():
-        for part in range(2):
-            kv_part(x, part, other_half, part).start()
-        kv_copy(sq, far_mate, 3).start()
-
-    for d in (2, 1, 3):
-        xt = lax.rem(x + d, NX)
-
-        @pl.when(xt > x)
-        def _():
-            kv_copy(sq, x_mate(xt), d - 1).start()
-
-    def li_copy(direction, n, arrived=False):
-        sign = 1 - 2 * direction
-        away = n // 2 + 1 if arrived else n // 2
-        half = direction if n == 6 else n % 2
-        ref = li_buf.at[lax.rem(hd - sign * away + NZ, NZ), pl.ds(16 * half, 16), :]
-        return remote(ref, ref, li_ss.at[direction, n], li_rs.at[direction, n], z_mate(sign))
-
-    def li_start(n):
-        for direction in range(2):
-            li_copy(direction, n).start()
-
-    def li_wait(n):
-        for direction in range(2):
-            li_copy(direction, n, True).wait_recv()
-
-    def li_next(n):
-        li_wait(n)
-        if n == 4:
-            li_copy(0, 6).start()
-        elif n == 5:
-            li_copy(1, 6).start()
-        else:
-            li_start(n + 2)
-
-    li_start(0)
-    li_start(1)
+
     li_next(0)
 
     @pl.when(y_hi == 1)
@@ -274,14 +277,14 @@
 
     @pl.when(y_hi == 1)
     def _():
+        grad_block(far_x)
+        far_copy.start()
+
         @pl.loop(0, 2)
         def _(n):
             grad_block(lax.rem(x + 1 + 2 * n, NX))
             for part in range(2):
                 c_copy(n, part).start()
-
-        grad_block(far_x)
-        far_copy.start()
 
     li_next(4)
 
@@ -314,8 +317,6 @@
 
     for g in range(GROUP):
         qg_out[:, g * HD : (g + 1) * HD] = dq_t[g].T.astype(BF)
-    qg_copy = pltpu.make_async_copy(qg_out, qg_hbm, out_sem.at[0])
-    qg_copy.start()
 
     for c in loads[10:]:
         c.wait()
@@ -472,24 +473,12 @@
             z_copy(direction, 3, half).wait_recv()
             term = term + zr[direction, 3, half].astype(F32)
         ig_out[:, half * HALF : (half + 1) * HALF] = term.astype(BF)
-    ig_copy = pltpu.make_async_copy(ig_out, ig_hbm, out_sem.at[1])
-    ig_copy.start()
-
-    def gp_copy(c, p):
-        return pltpu.make_async_copy(gfull.at[c, p], gp_hbm.at[c, p], gp_sem.at[c, p])
-
-    def part_done(p):
+
+    hand_over(2)
+    hand_over(3)
+    for p in range(PARTS):
         for d in range(NX):
             pair_copy(p, d, True).wait_recv()
-        for c in range(2):
-            gp_copy(c, p).start()
-
-    hand_over(2)
-    part_done(0)
-    part_done(1)
-    hand_over(3)
-    part_done(2)
-    part_done(3)
 
     for d in range(1, NX):
         xt = lax.rem(x + d, NX)
@@ -533,11 +522,6 @@
             ag_copy(p, d).wait_send()
         for d in range(NX):
             pair_copy(p, d).wait_send()
-    qg_copy.wait()
-    ig_copy.wait()
-    for p in range(PARTS):
-        for c in range(2):
-            gp_copy(c, p).wait()
 
 
 def finish(
@@ -593,15 +577,12 @@
         pltpu.VMEM((NZ, 32, D), F32),
         pltpu.VMEM((2, 4, 2, 32, HALF), BF),
         pltpu.VMEM((2, 4, 2, 32, HALF), BF),
-        pltpu.VMEM((32, D), BF),
         pltpu.VMEM((PARTS, PART, 2 * HD), BF),
         pltpu.VMEM((PARTS, PART, 2 * HD), BF),
         pltpu.VMEM((PARTS, NX, SUB, 2 * HD), F32),
         pltpu.VMEM((PARTS, NX, SUB, 2 * HD), BF),
         pltpu.VMEM((PARTS, NX - 1, SUB, 2 * HD), BF),
         pltpu.VMEM((PARTS, NX, SUB, 2 * HD), BF),
-        pltpu.VMEM((2, PARTS, NX, SUB, 2 * HD), BF),
-        pltpu.VMEM((ROWS, GROUP * HD), BF),
         dma((12,)),
         dma((NX,)),
         dma((NS,)),
@@ -627,8 +608,6 @@
         dma((PARTS, 3)),
         dma((PARTS, 4)),
         dma((PARTS, 4)),
-        dma((2,)),
-        dma((2, PARTS)),
     ]
     qg, ig, gp = pl.pallas_call(
         kernel,

time: 65.6 us -> 63.7 us (0.971)
  Pallas kernels: 64.9 us -> 63 us
    pallas_call x1, Pallas kernels: 63 us -> 61.1 us  [shards(): pl.pallas_call(kernel, out_shape=(pltpu.VMEM((ROWS, GROUP * HD), BF), plt...]
where the time goes in v6:
time: 63.7 us; the launch traced here: 63.6 us
  Pallas kernels  63 us (99%)
  between operations  0.64 us (1%)
    pallas_call x1, Pallas kernels, shards(): pl.pallas_call(kernel, out_shape=(pltpu.VMEM((ROWS, GROUP * HD), BF), plt...  61.1 us
    pallas_call x1, Pallas kernels, shards(): pl.pallas_call(finish, out_shape=(jax.ShapeDtypeStruct((ROWS, GROUP * HD)...  1.88 us

profile of v6, /device:TPU:1, one launch (start us, length us, event | category | flops | bytes accessed | tf_op | source)
XLA Modules:
  0.0 63.6 jit_solution(8374615303310730)
XLA Ops:
  0.6 61.1 %shard_map.111 = (bf16[256,384]{1,0:T(8,128)(2,1)S(1)}, bf16[32,3072]{1,0:T(8,128)(2,1)S(1)}, bf16[2,4,4,96,256]{4,3,2,1,0:T(8,128)(2,1)S(1)}) custom-call(bf16[256,384]{1,0:T(8,128)(2,1)} %bitcast.9, bf16[256,128]{1,0:T(8,128)(2,1)} %bitcast.14, bf16[256,128]{1,0:T(8,128)(2,1)} %bitcast.15, bf16[256,384]{1,0:T(8,128)(2,1)} %bitcast.10, s32[1,256]{1,0:T(1,128)} %docs_hbm.1, ...), custom_call_target="tpu_custom_call" | custom-call | flops 3000000000 | bytes 8000000 | tf_op jit(solution)/shard_map/pallas_call | solution.py:612
  61.7 1.9 %shard_map.112 = (bf16[256,384]{1,0:T(8,128)(2,1)}, bf16[32,3072]{1,0:T(8,128)(2,1)}, f32[3072,128]{1,0:T(8,128)}, f32[3072,128]{1,0:T(8,128)}) custom-call(bf16[256,384]{1,0:T(8,128)(2,1)S(1)} %get-tuple-element.11.qg_in, bf16[32,3072]{1,0:T(8,128)(2,1)S(1)} %get-tuple-element.12.ig_in, bf16[3072,256]{1,0:T(8,128)(2,1)S(1)} %bitcast.8), custom_call_target="tpu_custom_call" | custom-call | bytes 6000000 | tf_op jit(solution)/shard_map/pallas_call | solution.py:633

commit v7 on v6

--- a/solution.py
+++ b/solution.py
@@ -194,14 +194,14 @@
 
     score_block(sq, True)
 
-    li_next(0)
-
     @pl.when(y_hi == 1)
     def _():
         for part in range(2):
             kv_part(x, part, other_half, 0).wait_recv()
             for n, d in enumerate((1, 3)):
                 kv_part(x, part, x_mate(lax.rem(x + d, NX)), 2 + 2 * part + n).start()
+
+    li_next(0)
 
     @pl.loop(1, NX)
     def _(d):

time: 63.7 us -> 63.7 us (level)
  no operation moved by 1% of the time
where the time goes in v7:
time: 63.7 us; the launch traced here: 63.6 us
  Pallas kernels  63 us (99%)
  between operations  0.64 us (1%)
    pallas_call x1, Pallas kernels, shards(): pl.pallas_call(kernel, out_shape=(pltpu.VMEM((ROWS, GROUP * HD), BF), plt...  61.1 us
    pallas_call x1, Pallas kernels, shards(): pl.pallas_call(finish, out_shape=(jax.ShapeDtypeStruct((ROWS, GROUP * HD)...  1.88 us

profile of v7, /device:TPU:1, one launch (start us, length us, event | category | flops | bytes accessed | tf_op | source)
XLA Modules:
  0.0 63.6 jit_solution(7841545840504606077)
XLA Ops:
  0.6 61.1 %shard_map.111 = (bf16[256,384]{1,0:T(8,128)(2,1)S(1)}, bf16[32,3072]{1,0:T(8,128)(2,1)S(1)}, bf16[2,4,4,96,256]{4,3,2,1,0:T(8,128)(2,1)S(1)}) custom-call(bf16[256,384]{1,0:T(8,128)(2,1)} %bitcast.9, bf16[256,128]{1,0:T(8,128)(2,1)} %bitcast.14, bf16[256,128]{1,0:T(8,128)(2,1)} %bitcast.15, bf16[256,384]{1,0:T(8,128)(2,1)} %bitcast.10, s32[1,256]{1,0:T(1,128)} %docs_hbm.1, ...), custom_call_target="tpu_custom_call" | custom-call | flops 3000000000 | bytes 8000000 | tf_op jit(solution)/shard_map/pallas_call | solution.py:612
  61.8 1.9 %shard_map.112 = (bf16[256,384]{1,0:T(8,128)(2,1)}, bf16[32,3072]{1,0:T(8,128)(2,1)}, f32[3072,128]{1,0:T(8,128)}, f32[3072,128]{1,0:T(8,128)}) custom-call(bf16[256,384]{1,0:T(8,128)(2,1)S(1)} %get-tuple-element.11.qg_in, bf16[32,3072]{1,0:T(8,128)(2,1)S(1)} %get-tuple-element.12.ig_in, bf16[3072,256]{1,0:T(8,128)(2,1)S(1)} %bitcast.8), custom_call_target="tpu_custom_call" | custom-call | bytes 6000000 | tf_op jit(solution)/shard_map/pallas_call | solution.py:633

commit v8 on v6

--- a/solution.py
+++ b/solution.py
@@ -77,7 +77,7 @@
     barrier = pltpu.get_barrier_semaphore()
     partners = [x_mate(lax.rem(x + d, NX)) for d in range(1, NX)]
     partners += [y_mate(lax.rem(yi + d, NX)) for d in range(1, NX)]
-    partners += [far_mate, other_core, z_mate(1), z_mate(-1)]
+    partners += [other_core, z_mate(1), z_mate(-1)]
     for dev in partners:
         pl.semaphore_signal(barrier, inc=1, device_id=dev, device_id_type=pl.DeviceIdType.MESH)
 
@@ -127,12 +127,12 @@
     def _():
         for part in range(2):
             kv_part(x, part, other_half, part).start()
-        kv_copy(sq, far_mate, 3).start()
+        kv_copy(sq, x_mate(far_x), 1).start()
 
     for d in (2, 1, 3):
         xt = lax.rem(x + d, NX)
 
-        @pl.when(xt > x)
+        @pl.when((xt > x) & ((y_hi == 1) if d == 2 else True))
         def _():
             kv_copy(sq, x_mate(xt), d - 1).start()
 
@@ -196,6 +196,11 @@
 
     li_next(0)
 
+    @pl.when(y_hi == 0)
+    def _():
+        kv_arrived(far_x).wait_recv()
+        kv_copy(far_x, other_half, 3).start()
+
     @pl.when(y_hi == 1)
     def _():
         for part in range(2):
@@ -207,7 +212,10 @@
     def _(d):
         @pl.when(d <= x)
         def _():
-            kv_arrived(sq - d).wait_recv()
+            @pl.when((y_hi == 1) | (d != 2))
+            def _():
+                kv_arrived(sq - d).wait_recv()
+
             score_block(sq - d, False)
 
     li_next(1)
@@ -411,9 +419,9 @@
         ref = gfull.at[core, p, lax.rem(own - d + NX, NX) if arrived else own]
         return remote(ref, ref, ag_ss.at[p, d - 1], ag_rs.at[p, d - 1], mate(p % 2, d))
 
-    def pair_copy(p, d, arrived=False):
-        ref = gfull.at[1 - core if arrived else core, p, lax.rem(index(p % 2) - d + NX, NX)]
-        return remote(ref, ref, p_ss.at[p, d], p_rs.at[p, d], other_core)
+    def pair_copy(p, arrived=False):
+        ref = gfull.at[1 - core if arrived else core, p]
+        return remote(ref, ref, p_ss.at[p], p_rs.at[p], other_core)
 
     for p in range(PARTS):
         h32[p] = proj_part(core, p).reshape(NX, SUB, 2 * HD)
@@ -444,12 +452,11 @@
         gfull[core, p, index(p % 2)] = term.astype(BF)
         for d in (2, 1, 3):
             ag_copy(p, d).start()
-        pair_copy(p, 0).start()
 
     def hand_over(p):
         for d in (1, 3, 2):
             ag_copy(p, d, True).wait_recv()
-            pair_copy(p, d).start()
+        pair_copy(p).start()
 
     z_step(1, 0)
     stage2(0)
@@ -477,13 +484,12 @@
     hand_over(2)
     hand_over(3)
     for p in range(PARTS):
-        for d in range(NX):
-            pair_copy(p, d, True).wait_recv()
+        pair_copy(p, True).wait_recv()
 
     for d in range(1, NX):
         xt = lax.rem(x + d, NX)
 
-        @pl.when(xt > x)
+        @pl.when((xt > x) & ((y_hi == 1) if d == 2 else True))
         def _():
             kv_copy(sq, x_mate(xt), d - 1).wait_send()
 
@@ -495,7 +501,8 @@
     def _():
         for part in range(2):
             kv_part(x, part, other_half, part).wait_send()
-        kv_copy(sq, far_mate, 3).wait_send()
+        kv_copy(sq, x_mate(far_x), 1).wait_send()
+        kv_copy(far_x, other_half, 3).wait_send()
 
     @pl.when(y_hi == 1)
     def _():
@@ -520,8 +527,7 @@
             st1_copy(p, d).wait_send()
             st2_copy(p, d).wait_send()
             ag_copy(p, d).wait_send()
-        for d in range(NX):
-            pair_copy(p, d).wait_send()
+        pair_copy(p).wait_send()
 
 
 def finish(
@@ -606,8 +612,8 @@
         dma((PARTS, 3)),
         dma((PARTS, 3)),
         dma((PARTS, 3)),
-        dma((PARTS, 4)),
-        dma((PARTS, 4)),
+        dma((PARTS,)),
+        dma((PARTS,)),
     ]
     qg, ig, gp = pl.pallas_call(
         kernel,

time: 63.7 us -> 63.8 us (level)
  no operation moved by 1% of the time
where the time goes in v8:
time: 63.8 us; the launch traced here: 63.7 us
  Pallas kernels  63.1 us (99%)
  between operations  0.64 us (1%)
    pallas_call x1, Pallas kernels, shards(): pl.pallas_call(kernel, out_shape=(pltpu.VMEM((ROWS, GROUP * HD), BF), plt...  61.2 us
    pallas_call x1, Pallas kernels, shards(): pl.pallas_call(finish, out_shape=(jax.ShapeDtypeStruct((ROWS, GROUP * HD)...  1.88 us

profile of v8, /device:TPU:1, one launch (start us, length us, event | category | flops | bytes accessed | tf_op | source)
XLA Modules:
  0.0 63.7 jit_solution(8559955278000041553)
XLA Ops:
  0.6 61.2 %shard_map.111 = (bf16[256,384]{1,0:T(8,128)(2,1)S(1)}, bf16[32,3072]{1,0:T(8,128)(2,1)S(1)}, bf16[2,4,4,96,256]{4,3,2,1,0:T(8,128)(2,1)S(1)}) custom-call(bf16[256,384]{1,0:T(8,128)(2,1)} %bitcast.9, bf16[256,128]{1,0:T(8,128)(2,1)} %bitcast.14, bf16[256,128]{1,0:T(8,128)(2,1)} %bitcast.15, bf16[256,384]{1,0:T(8,128)(2,1)} %bitcast.10, s32[1,256]{1,0:T(1,128)} %docs_hbm.1, ...), custom_call_target="tpu_custom_call" | custom-call | flops 3000000000 | bytes 8000000 | tf_op jit(solution)/shard_map/pallas_call | solution.py:618
  61.8 1.9 %shard_map.112 = (bf16[256,384]{1,0:T(8,128)(2,1)}, bf16[32,3072]{1,0:T(8,128)(2,1)}, f32[3072,128]{1,0:T(8,128)}, f32[3072,128]{1,0:T(8,128)}) custom-call(bf16[256,384]{1,0:T(8,128)(2,1)S(1)} %get-tuple-element.11.qg_in, bf16[32,3072]{1,0:T(8,128)(2,1)S(1)} %get-tuple-element.12.ig_in, bf16[3072,256]{1,0:T(8,128)(2,1)S(1)} %bitcast.8), custom_call_target="tpu_custom_call" | custom-call | bytes 6000000 | tf_op jit(solution)/shard_map/pallas_call | solution.py:639
